TPU v7x, 32 devices: a whole 2x2x4 slice. The times are simulated.
32 devices in a mesh: replica: 2 (over y), group: 16 (over z, x, core).
Axes of the slice: x: 2, y: 2, z: 4, core: 2. Of those that a mesh axis runs over, the one named last changes fastest.
Arguments:
- tokens: bfloat16 [4, 4096, 640], P('replica', 'group'), may hold values from -6 to 6
- cotangent: bfloat16 [4, 4096, 640], P('replica', 'group'), may hold values from -6 to 6
- lengths: int32 [4, 2], P('replica'), may hold values from 1 to 3072, 4096 in all within a row
- w_qkv: float32 [640, 1536], P('group'), may hold values from -0.25 to 0.25
- w_out: float32 [1024, 640], P('group'), may hold values from -0.1875 to 0.1875
- w_gu: float32 [640, 4096], P('group'), may hold values from -0.25 to 0.25
- w_down: float32 [2048, 640], P('group'), may hold values from -0.125 to 0.125
- norm_gains: float32 [3072], P('group'), may hold values from 0.5 to 1.5
- first_qkv: float32 [640, 1536], P('group'), may hold values from -80 to 80
- first_out: float32 [1024, 640], P('group'), may hold values from -80 to 80
- first_gu: float32 [640, 4096], P('group'), may hold values from -56 to 56
- first_down: float32 [2048, 640], P('group'), may hold values from -80 to 80
- first_gains: float32 [3072], P('group'), may hold values from -128 to 128
- second_qkv: float32 [640, 1536], P('group'), may hold values from 19.6608 to 81.92
- second_out: float32 [1024, 640], P('group'), may hold values from 16.384 to 65.536
- second_gu: float32 [640, 4096], P('group'), may hold values from 6.5536 to 26.2144
- second_down: float32 [2048, 640], P('group'), may hold values from 16.384 to 65.536
- second_gains: float32 [3072], P('group'), may hold values from 36.0448 to 147.456
Outputs:
- layer_out: bfloat16 [4, 4096, 640], P('replica', 'group')
- token_grad: float32 [4, 4096, 640], P('replica', 'group')
- moment_qkv: float32 [640, 1536], P('group')
- square_qkv: float32 [640, 1536], P('group')
- master_qkv: float32 [640, 1536], P('group')
- moment_out: float32 [1024, 640], P('group')
- square_out: float32 [1024, 640], P('group')
- master_out: float32 [1024, 640], P('group')
- moment_gu: float32 [640, 4096], P('group')
- square_gu: float32 [640, 4096], P('group')
- master_gu: float32 [640, 4096], P('group')
- moment_down: float32 [2048, 640], P('group')
- square_down: float32 [2048, 640], P('group')
- master_down: float32 [2048, 640], P('group')
- moment_gains: float32 [3072], P('group')
- square_gains: float32 [3072], P('group')
- master_gains: float32 [3072], P('group')
Inputs may be any that keep to these rules, and one draw needn't show every extreme that they name: Each row holds two sequences whose lengths sum to 4096.
All inputs are finite; a program needn't handle non-finite values.
Results may differ from a plain program's by a relative error of at most 0.035.
Values may be sent and summed in bfloat16 or wider, within the bound.
No kernel may reach another device: no remote copies, remote signals or barrier semaphores. Data moves between devices by JAX's collectives and lax.ppermute only.
A program may use at most 256 MiB of HBM per device.

v0:
```python
import math

import jax
import jax.numpy as jnp
from jax import lax
from jax.experimental import pallas as pl
from jax.experimental.pallas import tpu as pltpu
from jax.sharding import PartitionSpec as P

D = 640
HQ = 4
HD = 256
FF = 2048
SEG = 256
STEP = 10


EPS_NORM = 1e-06
BETA_ONE = 0.9
BETA_TWO = 0.999
ADAM_EPS = 1e-08
RATE_MATRIX = 0.1
RATE_GAIN = 0.5
DECAY_RATE = 0.1
ROPE_BASE = 1000000.0
NEGATIVE = -1e30
SCALE_SCORE = 0.0625


def rms_norm(values, gain_row):
    factor = lax.rsqrt(jnp.mean(values * values, axis=-1, keepdims=True) + EPS_NORM)
    return values * factor * gain_row


def angles(position, width):
    half_width = width // 2
    frequency = jnp.exp(
        jnp.arange(half_width, dtype=jnp.float32) * (-2.0 * math.log(ROPE_BASE) / width)
    )
    angle_table = position.astype(jnp.float32)[:, None] * frequency[None, :]
    return (jnp.cos(angle_table), jnp.sin(angle_table))


def rotate(values, cosine, sine):
    half_width = values.shape[-1] // 2
    leading = values[..., :half_width]
    trailing = values[..., half_width:]
    return jnp.concatenate(
        [leading * cosine - trailing * sine, trailing * cosine + leading * sine], axis=-1
    )


def layout(lengths, total):
    seq_ends = jnp.cumsum(lengths)
    seq_starts = seq_ends - lengths
    stream_index = jnp.arange(total, dtype=jnp.int32)
    segment = jnp.sum((stream_index[:, None] >= seq_ends[None, :]).astype(jnp.int32), axis=1)
    seq_begin = jnp.max(
        jnp.where(stream_index[:, None] >= seq_starts[None, :], seq_starts[None, :], 0), axis=1
    )
    return (segment, stream_index - seq_begin)


def head_in(values, gain_row, cosine, sine):
    return rotate(rms_norm(values, gain_row), cosine, sine)


def geglu(gate_up):
    return jax.nn.gelu(gate_up[:, :FF], approximate=True) * gate_up[:, FF:]


def split_gains(gain_all):
    return (
        gain_all[0:D],
        gain_all[D : 2 * D],
        gain_all[2 * D : 3 * D],
        gain_all[3 * D : 4 * D],
        gain_all[4 * D : 4 * D + HD],
        gain_all[4 * D + HD : 4 * D + 2 * HD],
    )


def adam_step(master, moment_one, moment_two, gradient, rate, decay):
    moment_new = BETA_ONE * moment_one + (1.0 - BETA_ONE) * gradient
    square_new = BETA_TWO * moment_two + (1.0 - BETA_TWO) * gradient * gradient
    moment_hat = moment_new / (1.0 - BETA_ONE**STEP)
    square_hat = square_new / (1.0 - BETA_TWO**STEP)
    master_new = master * (1.0 - rate * decay) - rate * moment_hat / (
        jnp.sqrt(square_hat) + ADAM_EPS
    )
    return (moment_new, square_new, master_new)


LOG2E = 1.4426950408889634
KEYS = 512
MEMBERS = 16
PACK = 32
HEAD = 24
REACH = 3
BLOCKS = 4 * REACH
NT = (((1,), (1,)), ((), ()))
TN = (((0,), (0,)), ((), ()))
F32 = jnp.float32
BF16 = jnp.bfloat16


def shift_z(values, k):
    return lax.ppermute(values, "group", [(i, (i + 4 * k) % MEMBERS) for i in range(MEMBERS)])


def line_up(values, lowest):
    return lax.ppermute(values, "group", [(i, i + 4) for i in range(4 * lowest, MEMBERS - 4)])


def line_down(values, lowest):
    return lax.ppermute(values, "group", [(i, i - 4) for i in range(4 * lowest, MEMBERS)])


def swap_x(values):
    return lax.ppermute(values, "group", [(i, i ^ 2) for i in range(MEMBERS)])


def swap_core(values):
    return lax.ppermute(values, "group", [(i, i ^ 1) for i in range(MEMBERS)])


def spread(lines):
    near = lines + [swap_x(line) for line in lines]
    return near + [swap_core(block) for block in near]


def gather_all(own):
    return spread([own] + [shift_z(own, k) for k in (1, 2, 3)])


def gather_keys(own, later):
    first = line_up(own, 0)
    second, over, over_first, later = lax.optimization_barrier(
        (line_up(first, 1), swap_x(own), swap_x(first), later)
    )
    near = [own, first, second, over, over_first, swap_x(second)]
    return near + [swap_core(block) for block in near], later


def scatter_keys(far, near_far, near):
    running = None
    for k in range(REACH - 1, -1, -1):
        came = swap_core(far[k]).astype(F32)
        over = swap_x((near_far[k].astype(F32) + came[1]).astype(BF16))
        total = near[k].astype(F32) + came[0] + over.astype(F32)
        if running is not None:
            total = total + running.astype(F32)
        if k:
            running = line_down(total.astype(BF16), k)
    return total


def scatter_x(near, came):
    return swap_x((near[4:].astype(F32) + came[4:].astype(F32)).astype(BF16))


def scatter_z(near, came, over):
    total = [near[k].astype(F32) + came[k].astype(F32) + over[k].astype(F32) for k in range(4)]
    for k in (1, 2, 3):
        total[0] = total[0] + shift_z(total[k].astype(BF16), k).astype(F32)
    return total[0].astype(BF16)


def over_replicas(shard):
    if lax.axis_size("replica") == 2:
        other = lax.ppermute(shard, "replica", [(0, 1), (1, 0)])
        return shard.astype(F32) + other.astype(F32)
    return lax.psum(shard, "replica").astype(F32)


def owner_up(info, place):
    cr, xr, k = place // 8, place // 4 % 2, place % 4
    return ((info[1] + k) & 3) * 4 + (info[2] ^ xr) * 2 + (info[3] ^ cr)


def order_kernel(info, *refs):
    blocks = refs[:MEMBERS]
    full_ref, rows = refs[MEMBERS], refs[-1]
    count = rows.shape[0] // MEMBERS
    for place in range(MEMBERS):
        cr, xr, k = place // 8, place // 4 % 2, place % 4
        owner = ((info[1] - k) & 3) * 4 + (info[2] ^ xr) * 2 + (info[3] ^ cr)
        values = blocks[place][...].astype(F32)
        rows[pl.ds(pl.multiple_of(owner * count, 8), count)] = values[:count]
        if len(refs) > MEMBERS + 2:
            refs[MEMBERS + 1][pl.ds(owner, 1)] = values[count : count + 1]
    full_ref[...] = rows[...].astype(BF16)


def order_rows(info, blocks, name):
    rows, columns = blocks[0].shape
    count = rows // 8 * 8
    vmem = pl.BlockSpec(memory_space=pltpu.VMEM)
    shapes = [jax.ShapeDtypeStruct((MEMBERS * count, columns), BF16)]
    if rows > count:
        shapes.append(jax.ShapeDtypeStruct((MEMBERS, columns), F32))
    return pl.pallas_call(
        order_kernel,
        out_shape=shapes,
        in_specs=[pl.BlockSpec(memory_space=pltpu.SMEM)] + [vmem] * MEMBERS,
        out_specs=[vmem] * len(shapes),
        scratch_shapes=[pltpu.VMEM((MEMBERS * count, columns), F32)],
        compiler_params=pltpu.CompilerParams(vmem_limit_bytes=32 * 1024 * 1024),
        cost_estimate=pl.CostEstimate(flops=0, bytes_accessed=4_000_000, transcendentals=0),
        name=name,
    )(info, *blocks)


def gradient_kernel(tile, pairs, extra, info, *refs):
    operands = refs[: 2 * pairs + extra]
    near, far = refs[2 * pairs + extra : 2 * pairs + extra + 2]
    sums = refs[2 * pairs + extra + 2 :]
    columns = near.shape[2]
    for begin in range(0, columns, tile):
        at = slice(begin, begin + tile)
        for pair in range(pairs):
            left, right = operands[2 * pair], operands[2 * pair + 1]
            sums[pair][...] = lax.dot_general(
                left[...], right[:, at], TN, preferred_element_type=F32
            )
        for place in range(MEMBERS):
            owner = owner_up(info, place)
            parts = []
            for pair in range(pairs):
                count = sums[pair].shape[0] // MEMBERS
                parts.append(sums[pair][pl.ds(pl.multiple_of(owner * count, 8), count)])
            if extra:
                row = operands[2 * pairs][pl.ds(owner, 1), at]
                parts.append(jnp.broadcast_to(row, (8, tile)))
            block = jnp.concatenate(parts, axis=0) if len(parts) > 1 else parts[0]
            target = far if place >= 8 else near
            target[place % 8, :, at] = block.astype(BF16)


def weight_gradient(info, pairs, gains, tile, name):
    columns = pairs[0][1].shape[1]
    tokens_here = pairs[0][0].shape[0]
    counts = [left.shape[1] // MEMBERS for left, _ in pairs]
    rows = sum(counts) + (8 if gains is not None else 0)
    operands = [operand for pair in pairs for operand in pair]
    if gains is not None:
        operands.append(gains)
    shape = jax.ShapeDtypeStruct((MEMBERS // 2, rows, columns), BF16)
    vmem = pl.BlockSpec(memory_space=pltpu.VMEM)
    return pl.pallas_call(
        lambda *refs: gradient_kernel(tile, len(pairs), int(gains is not None), *refs),
        out_shape=(shape, shape),
        in_specs=[pl.BlockSpec(memory_space=pltpu.SMEM)] + [vmem] * len(operands),
        out_specs=(vmem, vmem),
        scratch_shapes=[pltpu.VMEM((MEMBERS * count, tile), F32) for count in counts],
        compiler_params=pltpu.CompilerParams(vmem_limit_bytes=48 * 1024 * 1024),
        cost_estimate=pl.CostEstimate(
            flops=2 * tokens_here * columns * MEMBERS * sum(counts),
            bytes_accessed=4 * MEMBERS * rows * columns,
            transcendentals=0,
        ),
        name=name,
    )(info, *operands)


def pack_shards(out_shard, down_shard, gu_shard):
    mixed = jnp.concatenate([out_shard, down_shard], axis=0)
    rows, columns = mixed.shape
    tiles = mixed.reshape(rows // PACK, PACK, columns // 128, 128).transpose(1, 0, 2, 3)
    flat = tiles.reshape(PACK, -1)
    flat = jnp.pad(flat, ((0, 0), (0, gu_shard.shape[1] - flat.shape[1])))
    return jnp.concatenate([flat, gu_shard], axis=0)


def unpack_down(packed, rows):
    tiles = packed[:HEAD].reshape(HEAD // 8, 8, -1, 128).transpose(0, 2, 1, 3)
    count = rows // 8 * (D // 128)
    tiles = tiles.reshape(-1, 8, 128)[:count].reshape(rows // 8, D // 128, 8, 128)
    return tiles.transpose(0, 2, 1, 3).reshape(rows, D)


def unpack_kernel(packed, out_ref, down_ref, gu_ref):
    out_rows, down_rows = out_ref.shape[0] // 2, down_ref.shape[0] // 2
    for member in range(2):
        for i in range((out_rows + down_rows) // PACK):
            for j in range(D // 128):
                tile = 128 * (i * (D // 128) + j)
                values = packed[member, 0:PACK, tile : tile + 128]
                if i < out_rows // PACK:
                    row = member * out_rows + i * PACK
                    out_ref[row : row + PACK, 128 * j : 128 * j + 128] = values
                else:
                    row = member * down_rows + i * PACK - out_rows
                    down_ref[row : row + PACK, 128 * j : 128 * j + 128] = values
    for begin in range(0, 2 * FF, 1024):
        at = slice(begin, begin + 1024)
        both = [packed[member, PACK:, at].astype(F32) for member in range(2)]
        gu_ref[:, at] = jnp.concatenate(both, axis=0).astype(BF16)


def unpack_weights(packed):
    rows = packed.shape[1]
    out_rows, down_rows, gu_rows = HQ * HD // MEMBERS, FF // MEMBERS, rows - PACK
    return pl.pallas_call(
        unpack_kernel,
        grid=(MEMBERS // 2,),
        out_shape=(
            jax.ShapeDtypeStruct((HQ * HD, D), BF16),
            jax.ShapeDtypeStruct((FF, D), BF16),
            jax.ShapeDtypeStruct((MEMBERS * gu_rows, 2 * FF), BF16),
        ),
        in_specs=[pl.BlockSpec((2, rows, 2 * FF), lambda i: (i, 0, 0))],
        out_specs=(
            pl.BlockSpec((2 * out_rows, D), lambda i: (i, 0)),
            pl.BlockSpec((2 * down_rows, D), lambda i: (i, 0)),
            pl.BlockSpec((2 * gu_rows, 2 * FF), lambda i: (i, 0)),
        ),
        compiler_params=pltpu.CompilerParams(vmem_limit_bytes=32 * 1024 * 1024),
        cost_estimate=pl.CostEstimate(flops=0, bytes_accessed=19_000_000, transcendentals=0),
        name="unpack_weights",
    )(packed)


def feed_back_kernel(down, hidden, gate_up, ff, w_down, w_gu, db_ref, packed, dgu, sums):
    tile = 512
    root = math.sqrt(2.0 / math.pi)
    for begin in range(0, FF, tile):
        at = slice(begin, begin + tile)
        at_up = slice(FF + begin, FF + begin + tile)
        dh = lax.dot_general(down[...], w_down[at, :], NT, preferred_element_type=F32)
        gate, up = gate_up[:, at], gate_up[:, at_up]
        square = gate * gate
        wave = jnp.tanh(root * gate * (1.0 + 0.044715 * square))
        half = 0.5 * (1.0 + wave)
        slope = half + 0.5 * gate * (1.0 - wave * wave) * (root * (1.0 + 3.0 * 0.044715 * square))
        dgate = (dh * up * slope).astype(BF16)
        dup = (dh * gate * half).astype(BF16)
        dgu[:, at] = dgate
        dgu[:, at_up] = dup
        term = lax.dot_general(dgate, w_gu[:, at], NT, preferred_element_type=F32)
        term += lax.dot_general(dup, w_gu[:, at_up], NT, preferred_element_type=F32)
        if begin:
            db_ref[...] += term
        else:
            db_ref[...] = term
        sums[at, :] = lax.dot_general(hidden[:, at], down[...], TN, preferred_element_type=F32)
    gu_rows = packed.shape[1] - HEAD
    down_rows = FF // MEMBERS
    slabs = 2 * FF // 128
    for begin in range(0, 2 * FF, tile):
        block = lax.dot_general(
            ff[...], dgu[:, begin : begin + tile], TN, preferred_element_type=F32
        )
        for member in range(MEMBERS):
            lanes = []
            for slab in range(begin // 128, (begin + tile) // 128):
                parts = []
                for r in range(HEAD // 8):
                    i, j = divmod(r * slabs + slab, D // 128)
                    if 8 * i < down_rows:
                        row = member * down_rows + 8 * i
                        parts.append(sums[row : row + 8, 128 * j : 128 * j + 128])
                    else:
                        parts.append(jnp.zeros((8, 128), F32))
                lanes.append(jnp.concatenate(parts, axis=0))
            top = jnp.concatenate(lanes, axis=1)
            rows = block[member * gu_rows : (member + 1) * gu_rows]
            packed[member, :, begin : begin + tile] = jnp.concatenate([top, rows], axis=0).astype(
                BF16
            )


def feed_back(down, hidden, gate_up, ff, w_down, w_gu):
    vmem = pl.BlockSpec(memory_space=pltpu.VMEM)
    tokens_here = ff.shape[0]
    return pl.pallas_call(
        feed_back_kernel,
        out_shape=(
            jax.ShapeDtypeStruct((tokens_here, D), F32),
            jax.ShapeDtypeStruct((MEMBERS, HEAD + D // MEMBERS, 2 * FF), BF16),
        ),
        in_specs=[vmem] * 6,
        out_specs=(vmem, vmem),
        scratch_shapes=[pltpu.VMEM((tokens_here, 2 * FF), BF16), pltpu.VMEM((FF, D), F32)],
        compiler_params=pltpu.CompilerParams(vmem_limit_bytes=56 * 1024 * 1024),
        cost_estimate=pl.CostEstimate(
            flops=16 * tokens_here * D * FF, bytes_accessed=32_000_000, transcendentals=1_000_000
        ),
        name="feed_back",
    )(down, hidden, gate_up, ff, w_down, w_gu)


def key_range(info, stream):
    first = info[0]
    bound = info[4 + stream]
    low = jnp.where(first >= bound, bound, 0)
    high = jnp.where(first + SEG - 1 >= bound, bound, 0)
    return first, bound, low, high


def load_blocks(info, blocks, kv, sem):
    z, x, c = info[1], info[2], info[3]
    copies = []
    for place in range(len(blocks)):
        cr, xr, k = place // (2 * REACH), place // REACH % 2, place % REACH
        owner = ((z - k) & 3) * 4 + (x ^ xr) * 2 + (c ^ cr)
        copies.append(pltpu.make_async_copy(blocks[place], kv.at[owner], sem.at[place]))
    for copy in copies:
        copy.start()
    return copies


def forward_kernel(info, q_ref, *refs):
    blocks = refs[:BLOCKS]
    o_ref, lse_ref, kv, acc, total, sem = refs[BLOCKS:]
    copies = load_blocks(info, blocks, kv, sem)
    for copy in copies:
        copy.wait()

    def one_stream(stream, carry):
        mine = pl.ds(pl.multiple_of(stream * SEG, SEG), SEG)
        first, bound, low, high = key_range(info, stream)
        begin = low // KEYS
        diagonal = first // KEYS
        clear = jnp.clip((high + KEYS - 1) // KEYS, begin, diagonal)
        acc[...] = jnp.zeros_like(acc)
        total[...] = jnp.zeros_like(total)

        def visit(j, masked):
            keys = kv[pl.ds(2 * j, 2), stream, :, 0:HD].reshape(KEYS, HD)
            values = kv[pl.ds(2 * j, 2), stream, :, HD : 2 * HD].reshape(KEYS, HD)
            if masked:
                row = first + lax.broadcasted_iota(jnp.int32, (SEG, KEYS), 0)
                col = j * KEYS + lax.broadcasted_iota(jnp.int32, (SEG, KEYS), 1)
                mask = (col <= row) & (col >= jnp.where(row >= bound, bound, 0))
            for head in range(HQ):
                rows = slice(head * SEG, (head + 1) * SEG)
                query = q_ref[mine, head * HD : (head + 1) * HD]
                score = lax.dot_general(query, keys, NT, preferred_element_type=F32)
                prob = jnp.exp2(score * (SCALE_SCORE * LOG2E))
                if masked:
                    prob = jnp.where(mask, prob, 0.0)
                total[rows] += (
                    prob[:, 0:128] + prob[:, 128:256] + prob[:, 256:384] + prob[:, 384:512]
                )
                acc[rows] += jnp.dot(prob.astype(BF16), values, preferred_element_type=F32)

        def masked_step(i, carry):
            visit(jnp.where(i < clear, i, diagonal), True)
            return carry

        def clear_step(j, carry):
            visit(j, False)
            return carry

        lax.fori_loop(begin, clear + 1, masked_step, 0)
        lax.fori_loop(clear, diagonal, clear_step, 0)
        for head in range(HQ):
            rows = slice(head * SEG, (head + 1) * SEG)
            part = total[rows]
            out = acc[rows] / jnp.sum(part, axis=1, keepdims=True)
            o_ref[mine, head * HD : (head + 1) * HD] = out.astype(BF16)
            lse_ref[stream, :, rows] = jnp.log2(jnp.sum(part.T, axis=0, keepdims=True))
        return carry

    lax.fori_loop(0, 2, one_stream, 0)


def attention_forward(info, query, blocks):
    vmem = pl.BlockSpec(memory_space=pltpu.VMEM)
    return pl.pallas_call(
        forward_kernel,
        out_shape=(
            jax.ShapeDtypeStruct((2 * SEG, HQ * HD), BF16),
            jax.ShapeDtypeStruct((2, 1, HQ * SEG), F32),
        ),
        in_specs=[pl.BlockSpec(memory_space=pltpu.SMEM), vmem]
        + [pl.BlockSpec(memory_space=pl.ANY)] * BLOCKS,
        out_specs=(vmem, vmem),
        scratch_shapes=[
            pltpu.VMEM((MEMBERS, 2, SEG, 2 * HD), BF16),
            pltpu.VMEM((HQ * SEG, HD), F32),
            pltpu.VMEM((HQ * SEG, 128), F32),
            pltpu.SemaphoreType.DMA((BLOCKS,)),
        ],
        compiler_params=pltpu.CompilerParams(vmem_limit_bytes=40 * 1024 * 1024),
        cost_estimate=pl.CostEstimate(
            flops=7_000_000_000, bytes_accessed=9_000_000, transcendentals=7_000_000
        ),
        name="attention_forward",
    )(info, query, *blocks)


def backward_kernel(info, q_ref, o_ref, do_ref, lse_ref, *refs):
    blocks = refs[:BLOCKS]
    dq_ref = refs[BLOCKS]
    far = refs[BLOCKS + 1 : BLOCKS + 1 + REACH]
    near_far = refs[BLOCKS + 1 + REACH : BLOCKS + 1 + 2 * REACH]
    near = refs[BLOCKS + 1 + 2 * REACH : BLOCKS + 1 + 3 * REACH]
    kv, dkv, qs, qt, dos, dot_, dqt, delta, sem, out_sem = refs[BLOCKS + 1 + 3 * REACH :]
    copies = load_blocks(info, blocks, kv, sem)
    z, x, c = info[1], info[2], info[3]

    def clean(place, carry):
        dkv[place] = jnp.zeros((2, SEG, 2 * HD), BF16)
        return carry

    lax.fori_loop(0, BLOCKS, clean, 0)
    for copy in copies:
        copy.wait()

    def one_stream(stream, carry):
        first, bound, low, _ = key_range(info, stream)
        mine = pl.ds(pl.multiple_of(stream * SEG, SEG), SEG)
        for head in range(HQ):
            rows = slice(head * SEG, (head + 1) * SEG)
            lanes = slice(head * HD, (head + 1) * HD)
            query = q_ref[mine, lanes]
            grad = do_ref[mine, lanes]
            qs[rows] = query
            dos[rows] = grad
            qt[:, rows] = query.T
            dot_[:, rows] = grad.T
            both = grad.astype(F32) * o_ref[mine, lanes].astype(F32)
            delta[:, rows] = jnp.sum((both[:, 0:128] + both[:, 128:256]).T, axis=0, keepdims=True)
        dqt[...] = jnp.zeros_like(dqt)
        shape = (SEG, HQ * SEG)

        def visit(j, carry):
            keys = kv[j, stream, :, 0:HD]
            values = kv[j, stream, :, HD : 2 * HD]
            score = jnp.dot(keys, qt[...], preferred_element_type=F32)
            prob = jnp.exp2(score * (SCALE_SCORE * LOG2E) - lse_ref[stream])
            row = first + (lax.broadcasted_iota(jnp.int32, (1, HQ * SEG), 1) & (SEG - 1))
            start = jnp.where(row >= bound, bound, 0)
            col = j * SEG + lax.broadcasted_iota(jnp.int32, shape, 0)
            prob = jnp.where((col <= row) & (col >= start), prob, 0.0)
            dprob = jnp.dot(values, dot_[...], preferred_element_type=F32)
            dscore = (prob * (dprob - delta[...])).astype(BF16)
            dv = jnp.dot(prob.astype(BF16), dos[...], preferred_element_type=F32)
            dk = jnp.dot(dscore, qs[...], preferred_element_type=F32)
            dqt[...] += jnp.dot(keys.T, dscore, preferred_element_type=F32)
            place = ((j & 1) ^ c) * (2 * REACH) + (z - (j >> 2)) * 2 + (((j >> 1) & 1) ^ x)
            dkv[place, stream, :, 0:HD] = (dk * SCALE_SCORE).astype(BF16)
            dkv[place, stream, :, HD : 2 * HD] = dv.astype(BF16)
            return carry

        lax.fori_loop(low // SEG, first // SEG + 1, visit, 0)
        for head in range(HQ):
            rows = slice(head * SEG, (head + 1) * SEG)
            dq_ref[mine, head * HD : (head + 1) * HD] = dqt[:, rows].T * SCALE_SCORE
        return carry

    lax.fori_loop(0, 2, one_stream, 0)
    outs = []
    for k in range(REACH):
        outs.append((dkv.at[pl.ds(2 * REACH + 2 * k, 2)], far[k]))
        outs.append((dkv.at[2 * k + 1], near_far[k]))
        outs.append((dkv.at[2 * k], near[k]))
    copies = [
        pltpu.make_async_copy(source, target, out_sem.at[n])
        for n, (source, target) in enumerate(outs)
    ]
    for copy in copies:
        copy.start()
    for copy in copies:
        copy.wait()


def attention_backward(info, query, out, grad_out, lse, blocks):
    one = jax.ShapeDtypeStruct((2, SEG, 2 * HD), BF16)
    two = jax.ShapeDtypeStruct((2, 2, SEG, 2 * HD), BF16)
    vmem = pl.BlockSpec(memory_space=pltpu.VMEM)
    anywhere = pl.BlockSpec(memory_space=pl.ANY)
    result = pl.pallas_call(
        backward_kernel,
        out_shape=[jax.ShapeDtypeStruct((2 * SEG, HQ * HD), F32)]
        + [two] * REACH
        + [one] * (2 * REACH),
        in_specs=[pl.BlockSpec(memory_space=pltpu.SMEM)] + [vmem] * 4 + [anywhere] * BLOCKS,
        out_specs=[vmem] + [anywhere] * (3 * REACH),
        scratch_shapes=[
            pltpu.VMEM((MEMBERS, 2, SEG, 2 * HD), BF16),
            pltpu.VMEM((BLOCKS, 2, SEG, 2 * HD), BF16),
            pltpu.VMEM((HQ * SEG, HD), BF16),
            pltpu.VMEM((HD, HQ * SEG), BF16),
            pltpu.VMEM((HQ * SEG, HD), BF16),
            pltpu.VMEM((HD, HQ * SEG), BF16),
            pltpu.VMEM((HD, HQ * SEG), F32),
            pltpu.VMEM((1, HQ * SEG), F32),
            pltpu.SemaphoreType.DMA((BLOCKS,)),
            pltpu.SemaphoreType.DMA((3 * REACH,)),
        ],
        compiler_params=pltpu.CompilerParams(vmem_limit_bytes=52 * 1024 * 1024),
        cost_estimate=pl.CostEstimate(
            flops=17_000_000_000, bytes_accessed=20_000_000, transcendentals=7_000_000
        ),
        name="attention_backward",
    )(info, query, out, grad_out, lse, *blocks)
    return result[0], result[1 : 1 + REACH], result[1 + REACH : 1 + 2 * REACH], result[1 + 2 * REACH :]


def per_device(
    tokens,
    cotangent,
    lengths,
    w_qkv,
    w_out,
    w_gu,
    w_down,
    norm_gains,
    first_qkv,
    first_out,
    first_gu,
    first_down,
    first_gains,
    second_qkv,
    second_out,
    second_gu,
    second_down,
    second_gains,
):
    streams = tokens.shape[0]
    row_count = streams * SEG
    member_index = lax.axis_index("group")
    tok_rows = tokens.reshape(row_count, D).astype(F32)
    grad_out = cotangent.reshape(row_count, D).astype(F32)
    start_row = member_index * SEG
    boundary = lengths[:, 0]
    info = jnp.concatenate(
        [
            jnp.stack([start_row, member_index // 4, member_index // 2 % 2, member_index % 2]),
            boundary,
        ]
    ).astype(jnp.int32)
    q_width = HQ * HD
    low_qkv = w_qkv.astype(BF16)
    gain_count = norm_gains.shape[0]
    gain_row = jnp.pad(norm_gains.astype(BF16), (0, 2 * HD - gain_count))
    full_kv, gain_rows = order_rows(
        info,
        gather_all(jnp.concatenate([low_qkv[:, q_width:], gain_row[None]], axis=0)),
        "order_kv",
    )
    full_gains = gain_rows[:, :gain_count].reshape(-1)
    gain_in, gain_pa, gain_pf, gain_po, gain_query, gain_key = split_gains(full_gains)
    out_rows = w_out.shape[0]
    down_rows = w_down.shape[0]
    full_out, full_down, full_gu = unpack_weights(
        lax.all_gather(
            pack_shards(w_out.astype(BF16), w_down.astype(BF16), w_gu.astype(BF16)),
            "group",
            axis=0,
            tiled=False,
        )
    )
    index_mine = start_row + jnp.arange(SEG, dtype=jnp.int32)
    position_mine = index_mine[None, :] - jnp.where(
        index_mine[None, :] >= boundary[:, None], boundary[:, None], 0
    )
    cosine, sine = angles(position_mine.reshape(row_count), HD)
    normed_in, pull_in = jax.vjp(rms_norm, tok_rows, gain_in)
    input_low = normed_in.astype(BF16)
    kv_rows = jnp.dot(input_low, full_kv, preferred_element_type=F32)
    key_rot, pull_key = jax.vjp(
        lambda rows, gain: head_in(rows, gain, cosine, sine), kv_rows[:, :HD], gain_key
    )
    kv_low = jnp.concatenate([key_rot.astype(BF16), kv_rows[:, HD:].astype(BF16)], axis=1)
    blocks, low_q = gather_keys(kv_low.reshape(streams, SEG, 2 * HD), low_qkv[:, :q_width])
    (full_q,) = order_rows(info, gather_all(low_q), "order_q")
    query_rows = jnp.dot(input_low, full_q, preferred_element_type=F32)
    query_rot, pull_query = [], []
    for head in range(HQ):
        rotated, pull = jax.vjp(
            lambda rows, gain: head_in(rows, gain, cosine, sine),
            query_rows[:, head * HD : (head + 1) * HD],
            gain_query,
        )
        query_rot.append(rotated.astype(BF16))
        pull_query.append(pull)
    query_low = jnp.concatenate(query_rot, axis=1)
    attn_low, lse = attention_forward(info, query_low, blocks)
    attn_proj = jnp.dot(attn_low, full_out, preferred_element_type=F32)
    post_attn, pull_attn = jax.vjp(rms_norm, attn_proj, gain_pa)
    middle = tok_rows + post_attn
    normed_ff, pull_ff = jax.vjp(rms_norm, middle, gain_pf)
    ff_low = normed_ff.astype(BF16)
    gate_up = jnp.dot(ff_low, full_gu, preferred_element_type=F32)
    hidden = geglu(gate_up)
    hidden_low = hidden.astype(BF16)
    down_proj = jnp.dot(hidden_low, full_down, preferred_element_type=F32)
    post_ff, pull_post = jax.vjp(rms_norm, down_proj, gain_po)
    layer_out = (middle + post_ff).astype(BF16).reshape(streams, SEG, D)
    grad_down, grad_gain_po = pull_post(grad_out)
    down_low = grad_down.astype(BF16)
    grad_normed_ff, packed = feed_back(down_low, hidden_low, gate_up, ff_low, full_down, full_gu)
    mine = lax.psum_scatter(packed, "group", scatter_dimension=0, tiled=False)
    grad_middle_ff, grad_gain_pf = pull_ff(grad_normed_ff)
    grad_middle = grad_out + grad_middle_ff
    grad_attn_proj, grad_gain_pa = pull_attn(grad_middle)
    proj_low = grad_attn_proj.astype(BF16)
    grad_attn_low = jnp.dot(proj_low, full_out.T, preferred_element_type=F32).astype(BF16)
    near_out, far_out = weight_gradient(info, [(attn_low, proj_low)], None, 640, "gradient_out")
    grad_attn_low, near_out = lax.optimization_barrier((grad_attn_low, near_out))
    came_out = swap_core(far_out)
    over_out = scatter_x(near_out, came_out)
    grad_query, far, near_far, near = attention_backward(
        info, query_low, attn_low, grad_attn_low, lse, blocks
    )
    grad_kv = scatter_keys(far, near_far, near).reshape(row_count, 2 * HD)
    grad_query_rows, grad_gain_q = [], 0.0
    for head in range(HQ):
        rows, gain = pull_query[head](grad_query[:, head * HD : (head + 1) * HD])
        grad_query_rows.append(rows.astype(BF16))
        grad_gain_q = grad_gain_q + gain
    query_grad_low = jnp.concatenate(grad_query_rows, axis=1)
    near_q, far_q = weight_gradient(
        info, [(input_low, query_grad_low)], None, 512, "gradient_q"
    )
    came_q = swap_core(far_q)
    over_q = scatter_x(near_q, came_q)
    grad_kv, over_q, over_out, mine = lax.optimization_barrier((grad_kv, over_q, over_out, mine))
    sum_out = over_replicas(scatter_z(near_out, came_out, over_out))
    sum_q = over_replicas(scatter_z(near_q, came_q, over_q))
    grad_key_rows, grad_gain_k = pull_key(grad_kv[:, :HD])
    kv_grad_low = jnp.concatenate(
        [grad_key_rows.astype(BF16), grad_kv[:, HD:].astype(BF16)], axis=1
    )
    grad_normed_in = jnp.dot(query_grad_low, full_q.T, preferred_element_type=F32) + jnp.dot(
        kv_grad_low, full_kv.T, preferred_element_type=F32
    )
    grad_tokens_in, grad_gain_in = pull_in(grad_normed_in)
    token_grad = (grad_middle + grad_tokens_in).reshape(streams, SEG, D)
    wgrad_gains = jnp.concatenate(
        [grad_gain_in, grad_gain_pa, grad_gain_pf, grad_gain_po, grad_gain_q, grad_gain_k]
    )
    gains_out = jnp.pad(
        wgrad_gains.reshape(MEMBERS, gain_count), ((0, 0), (0, 2 * HD - gain_count))
    )
    near_kv, far_kv = weight_gradient(
        info, [(input_low, kv_grad_low)], gains_out, 2 * HD, "gradient_kv"
    )
    came_kv = swap_core(far_kv)
    sum_kv = over_replicas(scatter_z(near_kv, came_kv, scatter_x(near_kv, came_kv)))
    shard_qkv = jnp.concatenate([sum_q, sum_kv[:-8]], axis=1)
    shard_gains = sum_kv[-1, :gain_count]
    sum_packed = over_replicas(mine)
    sum_gu = sum_packed[HEAD:]
    sum_down = unpack_down(sum_packed, down_rows)
    upd_qkv = adam_step(w_qkv, first_qkv, second_qkv, shard_qkv, RATE_MATRIX, DECAY_RATE)
    upd_out = adam_step(w_out, first_out, second_out, sum_out, RATE_MATRIX, DECAY_RATE)
    upd_gu = adam_step(w_gu, first_gu, second_gu, sum_gu, RATE_MATRIX, DECAY_RATE)
    upd_down = adam_step(w_down, first_down, second_down, sum_down, RATE_MATRIX, DECAY_RATE)
    upd_gains = adam_step(norm_gains, first_gains, second_gains, shard_gains, RATE_GAIN, 0.0)
    return (layer_out, token_grad, *upd_qkv, *upd_out, *upd_gu, *upd_down, *upd_gains)


def solution(mesh):
    in_specs = (
        P("replica", "group", None),
        P("replica", "group", None),
        P("replica", None),
        P("group", None),
        P("group", None),
        P("group", None),
        P("group", None),
        P("group"),
        P("group", None),
        P("group", None),
        P("group", None),
        P("group", None),
        P("group"),
        P("group", None),
        P("group", None),
        P("group", None),
        P("group", None),
        P("group"),
    )
    out_specs = (
        P("replica", "group", None),
        P("replica", "group", None),
        P("group", None),
        P("group", None),
        P("group", None),
        P("group", None),
        P("group", None),
        P("group", None),
        P("group", None),
        P("group", None),
        P("group", None),
        P("group", None),
        P("group", None),
        P("group", None),
        P("group"),
        P("group"),
        P("group"),
    )
    return jax.shard_map(
        per_device, mesh=mesh, in_specs=in_specs, out_specs=out_specs, check_vma=False
    )
```

profile of v0, /device:TPU:0, one launch (start us, length us, event | category | flops | bytes accessed | tf_op | source)
XLA Modules:
  0.0 388.3 jit_solution(9665462051992064729)
XLA Ops:
  11.4 3.1 collective-permute-start
  14.5 2.6 collective-permute-start.1
  18.4 1.5 collective-permute-start.3
  21.2 1.6 collective-permute-start.5
  25.0 2.2 collective-permute-done.5.refs_6_
  27.1 1.7 collective-permute-done.6.refs_7_
  35.3 1.7 collective-permute-start.15
  37.0 2.1 collective-permute-start.17
  39.2 15.0 %collective-permute-done.15.refs_1_ = bf16[2,256,512]{2,1,0:T(8,128)(2,1)S(1)} collective-permute-done((bf16[2,256,512]{2,1,0:T(8,128)(2,1)}, bf16[2,256,512]{2,1,0:T(8,128)(2,1)S(1)}, u32[]{:S(2)}, u32[]{:S(2)}) %collective-permute-start.15) | collective-permute-done | bytes 524320 | tf_op jit(solution)/shard_map/ppermute | solution.py:112
  54.9 1.9 collective-permute-start.18
  56.8 23.6 %collective-permute-done.18.refs_4_ = bf16[2,256,512]{2,1,0:T(8,128)(2,1)S(1)} collective-permute-done((bf16[2,256,512]{2,1,0:T(8,128)(2,1)S(1)}, bf16[2,256,512]{2,1,0:T(8,128)(2,1)S(1)}, u32[]{:S(2)}, u32[]{:S(2)}) %collective-permute-start.18) | collective-permute-done | bytes 524320 | tf_op jit(solution)/shard_map/ppermute | solution.py:120
  80.4 10.5 %collective-permute-start.19 = (bf16[40,1024]{1,0:T(8,128)(2,1)S(1)}, bf16[40,1024]{1,0:T(8,128)(2,1)S(1)}, u32[]{:S(2)}, u32[]{:S(2)}) collective-permute-start(bf16[40,1024]{1,0:T(8,128)(2,1)S(1)} %slice.352.refs_0_), channel_id=1, source_target_pairs={{0,4},{1,5},{2,6},{3,7},{4,8},{5,9},{6,10},{7,11},{8,12},{9,13},{1... | collective-permute-start | bytes 245768 | tf_op jit(solution)/shard_map/ppermute | solution.py:108
  90.9 2.9 collective-permute-start.20
  93.8 2.0 collective-permute-start.21
  95.8 2.1 collective-permute-start.22
  97.9 2.4 collective-permute-start.23
  100.3 3.6 collective-permute-done.20.refs_2_
  104.0 2.4 collective-permute-start.24
  107.0 2.4 collective-permute-done.24.refs_6_
  109.4 1.5 collective-permute-done.25.refs_7_
  112.2 1.7 collective-permute-start.34
  117.6 1.6 fusion.132
  124.1 2.2 collective-permute-done.34.refs_5_
  129.9 4.6 %attention_forward.1 = (bf16[512,1024]{1,0:T(8,128)(2,1)S(1)}, f32[2,1,1024]{2,1,0:T(1,128)S(1)}) custom-call(s32[6]{0:T(128)S(1)} %concatenate.42.info.refs_0_, bf16[512,1024]{1,0:T(8,128)(2,1)S(1)} %fusion.125.q_ref, bf16[2,256,512]{2,1,0:T(8,128)(2,1)} %bitcast.5.refs_0_, bf16[2,256,512]{2,1,0:T(8,128)(2,1)S(1)} %collective-permute-done.15.refs_1_, ...), custom_call_target="tpu_custom_call" | custom-call | flops 7000000000 | bytes 9000000 | tf_op jit(solution)/shard_map/attention_forward/pallas_call | solution.py:471
  140.5 3.7 copy-done
  148.0 3.4 fusion.166.gate_up
  151.4 1.7 fusion.8.hidden
  153.1 1.6 copy-done.25
  154.7 1.9 multiply_reduce_fusion.4
  157.7 1.6 fusion.12
  159.3 20.6 %feed_back.1 = (f32[512,640]{1,0:T(8,128)}, bf16[16,64,4096]{2,1,0:T(8,128)(2,1)}) custom-call(bf16[512,640]{1,0:T(8,128)(2,1)} %get-tuple-element.153.down, bf16[512,2048]{1,0:T(8,128)(2,1)} %copy-done.42, f32[512,4096]{1,0:T(8,128)} %copy-done.25, bf16[512,640]{1,0:T(8,128)(2,1)} %copy-done.39, bf16[2048,640]{1,0:T(8,128)(2,1)} %copy-done.8, ...), custom_call_target="tpu_custom_call" | custom-call | flops 10737418240 | bytes 32000000 | tf_op jit(solution)/shard_map/feed_back/pallas_call | solution.py:376
  179.9 2.8 multiply_reduce_fusion
  182.7 2.9 multiply_reduce_fusion.1
  187.9 1.7 gradient_out.1
  189.7 2.0 convolution_convert_fusion.do_ref
  191.7 11.8 %attention_backward.1 = (f32[512,1024]{1,0:T(8,128)}, bf16[2,2,256,512]{3,2,1,0:T(8,128)(2,1)}, bf16[2,2,256,512]{3,2,1,0:T(8,128)(2,1)}, bf16[2,2,256,512]{3,2,...) custom-call(s32[6]{0:T(128)S(1)} %concatenate.42.info.refs_0_, ...), custom_call_target="tpu_custom_call" | custom-call | flops 16999999488 | bytes 20000000 | tf_op jit(solution)/shard_map/attention_backward/pallas_call | solution.py:575
  203.5 2.5 collective-permute-start.41
  206.6 3.0 fusion.107
  213.4 7.1 %collective-permute-start.46 = (bf16[2,256,512]{2,1,0:T(8,128)(2,1)S(1)}, bf16[2,256,512]{2,1,0:T(8,128)(2,1)S(1)}, u32[]{:S(2)}, u32[]{:S(2)}) collective-permute-start(bf16[2,256,512]{2,1,0:T(8,128)(2,1)S(1)} %fusion.24), channel_id=1, source_target_pairs={{0,2},{1,3},{2,0},{3,1},{4,6},{5,7},{6,4},{7,5},{8,10},{9,11},{10,... | collective-permute-start | bytes 1572872 | tf_op jit(solution)/shard_map/ppermute | solution.py:120
  221.7 17.3 %collective-permute-done.46 = bf16[2,256,512]{2,1,0:T(8,128)(2,1)S(1)} collective-permute-done((bf16[2,256,512]{2,1,0:T(8,128)(2,1)S(1)}, bf16[2,256,512]{2,1,0:T(8,128)(2,1)S(1)}, u32[]{:S(2)}, u32[]{:S(2)}) %collective-permute-start.46) | collective-permute-done | bytes 524320 | tf_op jit(solution)/shard_map/ppermute | solution.py:120
  240.1 1.5 gradient_q.1
  242.2 1.5 convert_element_type.451
  244.7 2.5 collective-permute-start.42
  247.1 8.5 %collective-permute-done.44 = bf16[2,256,512]{2,1,0:T(8,128)(2,1)S(1)} collective-permute-done((bf16[2,256,512]{2,1,0:T(8,128)(2,1)S(1)}, bf16[2,256,512]{2,1,0:T(8,128)(2,1)S(1)}, u32[]{:S(2)}, u32[]{:S(2)}) %collective-permute-start.44) | collective-permute-done | bytes 524320 | tf_op jit(solution)/shard_map/ppermute | solution.py:120
  259.0 2.0 collective-permute-start.50
  262.0 11.4 %collective-permute-done.42 = bf16[2,256,512]{2,1,0:T(8,128)(2,1)} collective-permute-done((bf16[2,256,512]{2,1,0:T(8,128)(2,1)}, bf16[2,256,512]{2,1,0:T(8,128)(2,1)}, u32[]{:S(2)}, u32[]{:S(2)}) %collective-permute-start.42) | collective-permute-done | bytes 524320 | tf_op jit(solution)/shard_map/ppermute | solution.py:120
  273.5 18.0 %collective-permute-done.48 = bf16[2,256,512]{2,1,0:T(8,128)(2,1)} collective-permute-done((bf16[2,256,512]{2,1,0:T(8,128)(2,1)}, bf16[2,256,512]{2,1,0:T(8,128)(2,1)}, u32[]{:S(2)}, u32[]{:S(2)}) %collective-permute-start.48) | collective-permute-done | bytes 524320 | tf_op jit(solution)/shard_map/ppermute | solution.py:116
  291.4 2.9 fusion.38
  294.4 23.1 %reduce-scatter.2.cloned.1.call-done = bf16[1,64,4096]{2,1,0:T(8,128)(2,1)} async-done(((bf16[16,64,4096]{2,1,0:T(8,128)(2,1)}), bf16[1,64,4096]{2,1,0:T(8,128)(2,1)}) %reduce-scatter.2.cloned.1.call-update) | async-done | bytes 524304 | tf_op jit(solution)/shard_map/reduce_scatter | solution.py:697
  318.6 2.4 fusion.115
  323.1 2.3 fusion.19
  329.3 2.1 collective-permute-start.55
  331.4 2.0 collective-permute-start.54
  335.5 3.0 collective-permute-start.65
  338.5 2.8 fusion.14
  342.0 1.5 collective-permute-start.67
  345.1 3.5 collective-permute-done.64
  349.6 1.5 collective-permute-start.66
  351.2 6.6 %collective-permute-done.56 = bf16[40,1024]{1,0:T(8,128)(2,1)S(1)} collective-permute-done((bf16[40,1024]{1,0:T(8,128)(2,1)S(1)}, bf16[40,1024]{1,0:T(8,128)(2,1)S(1)}, u32[]{:S(2)}, u32[]{:S(2)}) %collective-permute-start.56) | collective-permute-done | bytes 81952 | tf_op jit(solution)/shard_map/ppermute | solution.py:171
  360.3 5.0 %collective-permute-done.58 = bf16[4,48,512]{2,1,0:T(8,128)(2,1)S(1)} collective-permute-done((bf16[4,48,512]{2,1,0:T(8,128)(2,1)S(1)}, bf16[4,48,512]{2,1,0:T(8,128)(2,1)S(1)}, u32[]{:S(2)}, u32[]{:S(2)}) %collective-permute-start.58) | collective-permute-done | bytes 196640 | tf_op jit(solution)/shard_map/ppermute | solution.py:120
  365.4 3.5 collective-permute-start.61
  370.4 1.5 divide_subtract_fusion
  372.0 1.9 collective-permute-done.60
  375.2 1.5 collective-permute-start.62
  (380 shorter events, 77.1 us)
Async XLA Ops:
  7.2 133.3 %all-gather.3.cloned.1.call-start = ((), (), s32[]{:S(2)}) async-start(), calls=%async_computation.2 | async-start | bytes 10027008 | tf_op jit(solution)/shard_map/all_gather | solution.py:650
  11.2 306.3 %reduce-scatter.2.cloned.1.call-start = ((), (), s32[]{:S(2)}) async-start(), calls=%async_computation.1 | async-start | bytes 8912896 | tf_op jit(solution)/shard_map/reduce_scatter | solution.py:697
  11.4 9.0 %collective-permute-start = (bf16[41,512]{1,0:T(8,128)(2,1)S(1)}, bf16[41,512]{1,0:T(8,128)(2,1)S(1)}, u32[]{:S(2)}, u32[]{:S(2)}) collective-permute-start(bf16[41,512]{1,0:T(8,128)(2,1)S(1)} %pad_maximum_fusion.5.refs_0_), channel_id=1, source_target_pairs={{0,4},{1,5},{2,6},{3,7},{4,8},{5,9},{6,10},{7,11},{8,12},{9,13},{1... | collective-permute-start | bytes 125960 | tf_op jit(solution)/shard_map/ppermute | solution.py:108
  14.5 6.5 %collective-permute-start.1 = (bf16[41,512]{1,0:T(8,128)(2,1)S(1)}, bf16[41,512]{1,0:T(8,128)(2,1)S(1)}, u32[]{:S(2)}, u32[]{:S(2)}) collective-permute-start(bf16[41,512]{1,0:T(8,128)(2,1)S(1)} %pad_maximum_fusion.5.refs_0_), channel_id=1, source_target_pairs={{0,8},{1,9},{2,10},{3,11},{4,12},{5,13},{6,14},{7,15},{8,0},{9,1},... | collective-permute-start | bytes 125960 | tf_op jit(solution)/shard_map/ppermute | solution.py:108
  17.1 4.1 %collective-permute-start.2 = (bf16[41,512]{1,0:T(8,128)(2,1)S(1)}, bf16[41,512]{1,0:T(8,128)(2,1)S(1)}, u32[]{:S(2)}, u32[]{:S(2)}) collective-permute-start(bf16[41,512]{1,0:T(8,128)(2,1)S(1)} %pad_maximum_fusion.5.refs_0_), channel_id=1, source_target_pairs={{0,12},{1,13},{2,14},{3,15},{4,0},{5,1},{6,2},{7,3},{8,4},{9,5},{1... | collective-permute-start | bytes 125960 | tf_op jit(solution)/shard_map/ppermute | solution.py:108
  18.4 4.4 %collective-permute-start.3 = (bf16[41,512]{1,0:T(8,128)(2,1)S(1)}, bf16[41,512]{1,0:T(8,128)(2,1)S(1)}, u32[]{:S(2)}, u32[]{:S(2)}) collective-permute-start(bf16[41,512]{1,0:T(8,128)(2,1)S(1)} %pad_maximum_fusion.5.refs_0_), channel_id=1, source_target_pairs={{0,2},{1,3},{2,0},{3,1},{4,6},{5,7},{6,4},{7,5},{8,10},{9,11},{10,... | collective-permute-start | bytes 125960 | tf_op jit(solution)/shard_map/ppermute | solution.py:120
  19.9 2.9 collective-permute-start.7
  20.3 4.6 %collective-permute-start.4 = (bf16[41,512]{1,0:T(8,128)(2,1)S(1)}, bf16[41,512]{1,0:T(8,128)(2,1)S(1)}, u32[]{:S(2)}, u32[]{:S(2)}) collective-permute-start(bf16[41,512]{1,0:T(8,128)(2,1)S(1)} %collective-permute-done.refs_1_), channel_id=1, source_target_pairs={{0,2},{1,3},{2,0},{3,1},{4,6},{5,7},{6,4},{7,5},{8,10},{9,11},{10,... | collective-permute-start | bytes 125960 | tf_op jit(solution)/shard_map/ppermute | solution.py:120
  21.0 7.8 %collective-permute-start.8 = (bf16[41,512]{1,0:T(8,128)(2,1)S(1)}, bf16[41,512]{1,0:T(8,128)(2,1)S(1)}, u32[]{:S(2)}, u32[]{:S(2)}) collective-permute-start(bf16[41,512]{1,0:T(8,128)(2,1)S(1)} %collective-permute-done.refs_1_), channel_id=1, source_target_pairs={{0,1},{1,0},{2,3},{3,2},{4,5},{5,4},{6,7},{7,6},{8,9},{9,8},{10,11... | collective-permute-start | bytes 125960 | tf_op jit(solution)/shard_map/ppermute | solution.py:124
  21.2 5.9 %collective-permute-start.5 = (bf16[41,512]{1,0:T(8,128)(2,1)S(1)}, bf16[41,512]{1,0:T(8,128)(2,1)S(1)}, u32[]{:S(2)}, u32[]{:S(2)}) collective-permute-start(bf16[41,512]{1,0:T(8,128)(2,1)S(1)} %collective-permute-done.1.refs_2_), channel_id=1, source_target_pairs={{0,2},{1,3},{2,0},{3,1},{4,6},{5,7},{6,4},{7,5},{8,10},{9,11},{10,... | collective-permute-start | bytes 125960 | tf_op jit(solution)/shard_map/ppermute | solution.py:120
  22.8 6.5 %collective-permute-start.9 = (bf16[41,512]{1,0:T(8,128)(2,1)S(1)}, bf16[41,512]{1,0:T(8,128)(2,1)S(1)}, u32[]{:S(2)}, u32[]{:S(2)}) collective-permute-start(bf16[41,512]{1,0:T(8,128)(2,1)S(1)} %collective-permute-done.1.refs_2_), channel_id=1, source_target_pairs={{0,1},{1,0},{2,3},{3,2},{4,5},{5,4},{6,7},{7,6},{8,9},{9,8},{10,11... | collective-permute-start | bytes 125960 | tf_op jit(solution)/shard_map/ppermute | solution.py:124
  22.8 6.0 %collective-permute-start.6 = (bf16[41,512]{1,0:T(8,128)(2,1)S(1)}, bf16[41,512]{1,0:T(8,128)(2,1)S(1)}, u32[]{:S(2)}, u32[]{:S(2)}) collective-permute-start(bf16[41,512]{1,0:T(8,128)(2,1)S(1)} %collective-permute-done.2.refs_3_), channel_id=1, source_target_pairs={{0,2},{1,3},{2,0},{3,1},{4,6},{5,7},{6,4},{7,5},{8,10},{9,11},{10,... | collective-permute-start | bytes 125960 | tf_op jit(solution)/shard_map/ppermute | solution.py:120
  25.0 4.5 %collective-permute-start.10 = (bf16[41,512]{1,0:T(8,128)(2,1)S(1)}, bf16[41,512]{1,0:T(8,128)(2,1)S(1)}, u32[]{:S(2)}, u32[]{:S(2)}) collective-permute-start(bf16[41,512]{1,0:T(8,128)(2,1)S(1)} %collective-permute-done.2.refs_3_), channel_id=1, source_target_pairs={{0,1},{1,0},{2,3},{3,2},{4,5},{5,4},{6,7},{7,6},{8,9},{9,8},{10,11... | collective-permute-start | bytes 125960 | tf_op jit(solution)/shard_map/ppermute | solution.py:124
  35.3 18.9 %collective-permute-start.15 = (bf16[2,256,512]{2,1,0:T(8,128)(2,1)}, bf16[2,256,512]{2,1,0:T(8,128)(2,1)S(1)}, u32[]{:S(2)}, u32[]{:S(2)}) collective-permute-start(bf16[2,256,512]{2,1,0:T(8,128)(2,1)} %bitcast.5.refs_0_), channel_id=1, source_target_pairs={{0,4},{1,5},{2,6},{3,7},{4,8},{5,9},{6,10},{7,11},{8,12},{9,13},{1... | collective-permute-start | bytes 1572872 | tf_op jit(solution)/shard_map/ppermute | solution.py:112
  37.0 19.7 %collective-permute-start.17 = (bf16[2,256,512]{2,1,0:T(8,128)(2,1)}, bf16[2,256,512]{2,1,0:T(8,128)(2,1)S(1)}, u32[]{:S(2)}, u32[]{:S(2)}) collective-permute-start(bf16[2,256,512]{2,1,0:T(8,128)(2,1)} %bitcast.5.refs_0_), channel_id=1, source_target_pairs={{0,2},{1,3},{2,0},{3,1},{4,6},{5,7},{6,4},{7,5},{8,10},{9,11},{10,... | collective-permute-start | bytes 1572872 | tf_op jit(solution)/shard_map/ppermute | solution.py:120
  54.2 2.6 collective-permute-start.16
  54.9 25.5 %collective-permute-start.18 = (bf16[2,256,512]{2,1,0:T(8,128)(2,1)S(1)}, bf16[2,256,512]{2,1,0:T(8,128)(2,1)S(1)}, u32[]{:S(2)}, u32[]{:S(2)}) collective-permute-start(bf16[2,256,512]{2,1,0:T(8,128)(2,1)S(1)} %collective-permute-done.15.refs_1_), channel_id=1, source_target_pairs={{0,2},{1,3},{2,0},{3,1},{4,6},{5,7},{6,4},{7,5},{8,10},{9,11},{10,... | collective-permute-start | bytes 1572872 | tf_op jit(solution)/shard_map/ppermute | solution.py:120
  80.4 17.5 %collective-permute-start.19 = (bf16[40,1024]{1,0:T(8,128)(2,1)S(1)}, bf16[40,1024]{1,0:T(8,128)(2,1)S(1)}, u32[]{:S(2)}, u32[]{:S(2)}) collective-permute-start(bf16[40,1024]{1,0:T(8,128)(2,1)S(1)} %slice.352.refs_0_), channel_id=1, source_target_pairs={{0,4},{1,5},{2,6},{3,7},{4,8},{5,9},{6,10},{7,11},{8,12},{9,13},{1... | collective-permute-start | bytes 245768 | tf_op jit(solution)/shard_map/ppermute | solution.py:108
  90.9 13.1 %collective-permute-start.20 = (bf16[40,1024]{1,0:T(8,128)(2,1)S(1)}, bf16[40,1024]{1,0:T(8,128)(2,1)S(1)}, u32[]{:S(2)}, u32[]{:S(2)}) collective-permute-start(bf16[40,1024]{1,0:T(8,128)(2,1)S(1)} %slice.352.refs_0_), channel_id=1, source_target_pairs={{0,8},{1,9},{2,10},{3,11},{4,12},{5,13},{6,14},{7,15},{8,0},{9,1},... | collective-permute-start | bytes 245768 | tf_op jit(solution)/shard_map/ppermute | solution.py:108
  93.8 12.6 %collective-permute-start.21 = (bf16[40,1024]{1,0:T(8,128)(2,1)S(1)}, bf16[40,1024]{1,0:T(8,128)(2,1)S(1)}, u32[]{:S(2)}, u32[]{:S(2)}) collective-permute-start(bf16[40,1024]{1,0:T(8,128)(2,1)S(1)} %slice.352.refs_0_), channel_id=1, source_target_pairs={{0,12},{1,13},{2,14},{3,15},{4,0},{5,1},{6,2},{7,3},{8,4},{9,5},{1... | collective-permute-start | bytes 245768 | tf_op jit(solution)/shard_map/ppermute | solution.py:108
  95.8 10.6 %collective-permute-start.22 = (bf16[40,1024]{1,0:T(8,128)(2,1)S(1)}, bf16[40,1024]{1,0:T(8,128)(2,1)S(1)}, u32[]{:S(2)}, u32[]{:S(2)}) collective-permute-start(bf16[40,1024]{1,0:T(8,128)(2,1)S(1)} %slice.352.refs_0_), channel_id=1, source_target_pairs={{0,2},{1,3},{2,0},{3,1},{4,6},{5,7},{6,4},{7,5},{8,10},{9,11},{10,... | collective-permute-start | bytes 245768 | tf_op jit(solution)/shard_map/ppermute | solution.py:120
  97.9 8.5 %collective-permute-start.26 = (bf16[40,1024]{1,0:T(8,128)(2,1)S(1)}, bf16[40,1024]{1,0:T(8,128)(2,1)S(1)}, u32[]{:S(2)}, u32[]{:S(2)}) collective-permute-start(bf16[40,1024]{1,0:T(8,128)(2,1)S(1)} %slice.352.refs_0_), channel_id=1, source_target_pairs={{0,1},{1,0},{2,3},{3,2},{4,5},{5,4},{6,7},{7,6},{8,9},{9,8},{10,11... | collective-permute-start | bytes 245768 | tf_op jit(solution)/shard_map/ppermute | solution.py:124
  97.9 9.0 %collective-permute-start.23 = (bf16[40,1024]{1,0:T(8,128)(2,1)S(1)}, bf16[40,1024]{1,0:T(8,128)(2,1)S(1)}, u32[]{:S(2)}, u32[]{:S(2)}) collective-permute-start(bf16[40,1024]{1,0:T(8,128)(2,1)S(1)} %collective-permute-done.19.refs_1_), channel_id=1, source_target_pairs={{0,2},{1,3},{2,0},{3,1},{4,6},{5,7},{6,4},{7,5},{8,10},{9,11},{10,... | collective-permute-start | bytes 245768 | tf_op jit(solution)/shard_map/ppermute | solution.py:120
  104.0 5.5 %collective-permute-start.24 = (bf16[40,1024]{1,0:T(8,128)(2,1)S(1)}, bf16[40,1024]{1,0:T(8,128)(2,1)S(1)}, u32[]{:S(2)}, u32[]{:S(2)}) collective-permute-start(bf16[40,1024]{1,0:T(8,128)(2,1)S(1)} %collective-permute-done.20.refs_2_), channel_id=1, source_target_pairs={{0,2},{1,3},{2,0},{3,1},{4,6},{5,7},{6,4},{7,5},{8,10},{9,11},{10,... | collective-permute-start | bytes 245768 | tf_op jit(solution)/shard_map/ppermute | solution.py:120
  106.3 4.6 %collective-permute-start.25 = (bf16[40,1024]{1,0:T(8,128)(2,1)S(1)}, bf16[40,1024]{1,0:T(8,128)(2,1)S(1)}, u32[]{:S(2)}, u32[]{:S(2)}) collective-permute-start(bf16[40,1024]{1,0:T(8,128)(2,1)S(1)} %collective-permute-done.21.refs_3_), channel_id=1, source_target_pairs={{0,2},{1,3},{2,0},{3,1},{4,6},{5,7},{6,4},{7,5},{8,10},{9,11},{10,... | collective-permute-start | bytes 245768 | tf_op jit(solution)/shard_map/ppermute | solution.py:120
  106.4 4.5 %collective-permute-start.27 = (bf16[40,1024]{1,0:T(8,128)(2,1)S(1)}, bf16[40,1024]{1,0:T(8,128)(2,1)S(1)}, u32[]{:S(2)}, u32[]{:S(2)}) collective-permute-start(bf16[40,1024]{1,0:T(8,128)(2,1)S(1)} %collective-permute-done.19.refs_1_), channel_id=1, source_target_pairs={{0,1},{1,0},{2,3},{3,2},{4,5},{5,4},{6,7},{7,6},{8,9},{9,8},{10,11... | collective-permute-start | bytes 245768 | tf_op jit(solution)/shard_map/ppermute | solution.py:124
  106.4 5.0 %collective-permute-start.28 = (bf16[40,1024]{1,0:T(8,128)(2,1)S(1)}, bf16[40,1024]{1,0:T(8,128)(2,1)S(1)}, u32[]{:S(2)}, u32[]{:S(2)}) collective-permute-start(bf16[40,1024]{1,0:T(8,128)(2,1)S(1)} %collective-permute-done.20.refs_2_), channel_id=1, source_target_pairs={{0,1},{1,0},{2,3},{3,2},{4,5},{5,4},{6,7},{7,6},{8,9},{9,8},{10,11... | collective-permute-start | bytes 245768 | tf_op jit(solution)/shard_map/ppermute | solution.py:124
  106.9 4.6 %collective-permute-start.29 = (bf16[40,1024]{1,0:T(8,128)(2,1)S(1)}, bf16[40,1024]{1,0:T(8,128)(2,1)S(1)}, u32[]{:S(2)}, u32[]{:S(2)}) collective-permute-start(bf16[40,1024]{1,0:T(8,128)(2,1)S(1)} %collective-permute-done.21.refs_3_), channel_id=1, source_target_pairs={{0,1},{1,0},{2,3},{3,2},{4,5},{5,4},{6,7},{7,6},{8,9},{9,8},{10,11... | collective-permute-start | bytes 245768 | tf_op jit(solution)/shard_map/ppermute | solution.py:124
  110.9 3.0 collective-permute-start.32
  111.4 2.5 collective-permute-start.33
  111.5 12.4 %collective-permute-start.35 = (bf16[2,256,512]{2,1,0:T(8,128)(2,1)}, bf16[2,256,512]{2,1,0:T(8,128)(2,1)S(1)}, u32[]{:S(2)}, u32[]{:S(2)}) collective-permute-start(bf16[2,256,512]{2,1,0:T(8,128)(2,1)} %bitcast.5.refs_0_), channel_id=1, source_target_pairs={{0,1},{1,0},{2,3},{3,2},{4,5},{5,4},{6,7},{7,6},{8,9},{9,8},{10,11... | collective-permute-start | bytes 1572872 | tf_op jit(solution)/shard_map/ppermute | solution.py:124
  111.9 17.9 %collective-permute-start.36 = (bf16[2,256,512]{2,1,0:T(8,128)(2,1)S(1)}, bf16[2,256,512]{2,1,0:T(8,128)(2,1)S(1)}, u32[]{:S(2)}, u32[]{:S(2)}) collective-permute-start(bf16[2,256,512]{2,1,0:T(8,128)(2,1)S(1)} %collective-permute-done.15.refs_1_), channel_id=1, source_target_pairs={{0,1},{1,0},{2,3},{3,2},{4,5},{5,4},{6,7},{7,6},{8,9},{9,8},{10,11... | collective-permute-start | bytes 1572872 | tf_op jit(solution)/shard_map/ppermute | solution.py:124
  112.2 14.1 %collective-permute-start.34 = (bf16[2,256,512]{2,1,0:T(8,128)(2,1)S(1)}, bf16[2,256,512]{2,1,0:T(8,128)(2,1)S(1)}, u32[]{:S(2)}, u32[]{:S(2)}) collective-permute-start(bf16[2,256,512]{2,1,0:T(8,128)(2,1)S(1)} %collective-permute-done.16.refs_2_), channel_id=1, source_target_pairs={{0,2},{1,3},{2,0},{3,1},{4,6},{5,7},{6,4},{7,5},{8,10},{9,11},{10,... | collective-permute-start | bytes 1572872 | tf_op jit(solution)/shard_map/ppermute | solution.py:120
  113.9 15.9 %collective-permute-start.37 = (bf16[2,256,512]{2,1,0:T(8,128)(2,1)S(1)}, bf16[2,256,512]{2,1,0:T(8,128)(2,1)S(1)}, u32[]{:S(2)}, u32[]{:S(2)}) collective-permute-start(bf16[2,256,512]{2,1,0:T(8,128)(2,1)S(1)} %collective-permute-done.16.refs_2_), channel_id=1, source_target_pairs={{0,1},{1,0},{2,3},{3,2},{4,5},{5,4},{6,7},{7,6},{8,9},{9,8},{10,11... | collective-permute-start | bytes 1572872 | tf_op jit(solution)/shard_map/ppermute | solution.py:124
  113.9 15.9 %collective-permute-start.38 = (bf16[2,256,512]{2,1,0:T(8,128)(2,1)S(1)}, bf16[2,256,512]{2,1,0:T(8,128)(2,1)S(1)}, u32[]{:S(2)}, u32[]{:S(2)}) collective-permute-start(bf16[2,256,512]{2,1,0:T(8,128)(2,1)S(1)} %collective-permute-done.17.refs_3_), channel_id=1, source_target_pairs={{0,1},{1,0},{2,3},{3,2},{4,5},{5,4},{6,7},{7,6},{8,9},{9,8},{10,11... | collective-permute-start | bytes 1572872 | tf_op jit(solution)/shard_map/ppermute | solution.py:124
  123.9 5.9 %collective-permute-start.39 = (bf16[2,256,512]{2,1,0:T(8,128)(2,1)S(1)}, bf16[2,256,512]{2,1,0:T(8,128)(2,1)S(1)}, u32[]{:S(2)}, u32[]{:S(2)}) collective-permute-start(bf16[2,256,512]{2,1,0:T(8,128)(2,1)S(1)} %collective-permute-done.18.refs_4_), channel_id=1, source_target_pairs={{0,1},{1,0},{2,3},{3,2},{4,5},{5,4},{6,7},{7,6},{8,9},{9,8},{10,11... | collective-permute-start | bytes 1572872 | tf_op jit(solution)/shard_map/ppermute | solution.py:124
  126.3 3.6 collective-permute-start.40
  203.5 38.6 %collective-permute-start.41 = (bf16[2,2,256,512]{3,2,1,0:T(8,128)(2,1)}, bf16[2,2,256,512]{3,2,1,0:T(8,128)(2,1)}, u32[]{:S(2)}, u32[]{:S(2)}) collective-permute-start(bf16[2,2,256,512]{3,2,1,0:T(8,128)(2,1)} %get-tuple-element.68), channel_id=1, source_target_pairs={{0,1},{1,0},{2,3},{3,2},{4,5},{5,4},{6,7},{7,6},{8,9},{9,8},{10,11... | collective-permute-start | bytes 3145736 | tf_op jit(solution)/shard_map/ppermute | solution.py:124
  206.1 15.1 %collective-permute-start.43 = (bf16[2,2,256,512]{3,2,1,0:T(8,128)(2,1)}, bf16[2,2,256,512]{3,2,1,0:T(8,128)(2,1)S(1)}, u32[]{:S(2)}, u32[]{:S(2)}) collective-permute-start(bf16[2,2,256,512]{3,2,1,0:T(8,128)(2,1)} %get-tuple-element.71), channel_id=1, source_target_pairs={{0,1},{1,0},{2,3},{3,2},{4,5},{5,4},{6,7},{7,6},{8,9},{9,8},{10,11... | collective-permute-start | bytes 3145736 | tf_op jit(solution)/shard_map/ppermute | solution.py:124
  206.1 6.8 %collective-permute-start.45 = (bf16[2,2,256,512]{3,2,1,0:T(8,128)(2,1)}, bf16[2,2,256,512]{3,2,1,0:T(8,128)(2,1)S(1)}, u32[]{:S(2)}, u32[]{:S(2)}) collective-permute-start(bf16[2,2,256,512]{3,2,1,0:T(8,128)(2,1)} %get-tuple-element.74), channel_id=1, source_target_pairs={{0,1},{1,0},{2,3},{3,2},{4,5},{5,4},{6,7},{7,6},{8,9},{9,8},{10,11... | collective-permute-start | bytes 3145736 | tf_op jit(solution)/shard_map/ppermute | solution.py:124
  213.4 25.6 %collective-permute-start.46 = (bf16[2,256,512]{2,1,0:T(8,128)(2,1)S(1)}, bf16[2,256,512]{2,1,0:T(8,128)(2,1)S(1)}, u32[]{:S(2)}, u32[]{:S(2)}) collective-permute-start(bf16[2,256,512]{2,1,0:T(8,128)(2,1)S(1)} %fusion.24), channel_id=1, source_target_pairs={{0,2},{1,3},{2,0},{3,1},{4,6},{5,7},{6,4},{7,5},{8,10},{9,11},{10,... | collective-permute-start | bytes 1572872 | tf_op jit(solution)/shard_map/ppermute | solution.py:120
  221.6 34.1 %collective-permute-start.44 = (bf16[2,256,512]{2,1,0:T(8,128)(2,1)S(1)}, bf16[2,256,512]{2,1,0:T(8,128)(2,1)S(1)}, u32[]{:S(2)}, u32[]{:S(2)}) collective-permute-start(bf16[2,256,512]{2,1,0:T(8,128)(2,1)S(1)} %fusion.29), channel_id=1, source_target_pairs={{0,2},{1,3},{2,0},{3,1},{4,6},{5,7},{6,4},{7,5},{8,10},{9,11},{10,... | collective-permute-start | bytes 1572872 | tf_op jit(solution)/shard_map/ppermute | solution.py:120
  239.2 16.5 %collective-permute-start.47 = (bf16[2,256,512]{2,1,0:T(8,128)(2,1)S(1)}, bf16[2,256,512]{2,1,0:T(8,128)(2,1)S(1)}, u32[]{:S(2)}, u32[]{:S(2)}) collective-permute-start(bf16[2,256,512]{2,1,0:T(8,128)(2,1)S(1)} %fusion.27), channel_id=1, source_target_pairs={{8,4},{9,5},{10,6},{11,7},{12,8},{13,9},{14,10},{15,11},{24,20},{2... | collective-permute-start | bytes 1572872 | tf_op jit(solution)/shard_map/ppermute | solution.py:116
  241.6 16.5 %collective-permute-start.49 = (bf16[8,40,1024]{2,1,0:T(8,128)(2,1)S(1)}, bf16[8,40,1024]{2,1,0:T(8,128)(2,1)S(1)}, u32[]{:S(2)}, u32[]{:S(2)}) collective-permute-start(bf16[8,40,1024]{2,1,0:T(8,128)(2,1)S(1)} %get-tuple-element.77), channel_id=1, source_target_pairs={{0,1},{1,0},{2,3},{3,2},{4,5},{5,4},{6,7},{7,6},{8,9},{9,8},{10,11... | collective-permute-start | bytes 1966088 | tf_op jit(solution)/shard_map/ppermute | solution.py:124
  241.7 19.4 %collective-permute-start.51 = (bf16[8,64,640]{2,1,0:T(8,128)(2,1)S(1)}, bf16[8,64,640]{2,1,0:T(8,128)(2,1)S(1)}, u32[]{:S(2)}, u32[]{:S(2)}) collective-permute-start(bf16[8,64,640]{2,1,0:T(8,128)(2,1)S(1)} %get-tuple-element.79), channel_id=1, source_target_pairs={{0,1},{1,0},{2,3},{3,2},{4,5},{5,4},{6,7},{7,6},{8,9},{9,8},{10,11... | collective-permute-start | bytes 1966088 | tf_op jit(solution)/shard_map/ppermute | solution.py:124
  244.7 28.8 %collective-permute-start.42 = (bf16[2,256,512]{2,1,0:T(8,128)(2,1)}, bf16[2,256,512]{2,1,0:T(8,128)(2,1)}, u32[]{:S(2)}, u32[]{:S(2)}) collective-permute-start(bf16[2,256,512]{2,1,0:T(8,128)(2,1)} %fusion.35), channel_id=1, source_target_pairs={{0,2},{1,3},{2,0},{3,1},{4,6},{5,7},{6,4},{7,5},{8,10},{9,11},{10,... | collective-permute-start | bytes 1572872 | tf_op jit(solution)/shard_map/ppermute | solution.py:120
  256.8 34.6 %collective-permute-start.48 = (bf16[2,256,512]{2,1,0:T(8,128)(2,1)}, bf16[2,256,512]{2,1,0:T(8,128)(2,1)}, u32[]{:S(2)}, u32[]{:S(2)}) collective-permute-start(bf16[2,256,512]{2,1,0:T(8,128)(2,1)} %fusion.33), channel_id=1, source_target_pairs={{4,0},{5,1},{6,2},{7,3},{8,4},{9,5},{10,6},{11,7},{12,8},{13,9},{1... | collective-permute-start | bytes 1572872 | tf_op jit(solution)/shard_map/ppermute | solution.py:116
  259.0 35.3 %collective-permute-start.50 = (bf16[4,40,1024]{2,1,0:T(8,128)(2,1)}, bf16[4,40,1024]{2,1,0:T(8,128)(2,1)}, u32[]{:S(2)}, u32[]{:S(2)}) collective-permute-start(bf16[4,40,1024]{2,1,0:T(8,128)(2,1)} %add_convert_fusion.2), channel_id=1, source_target_pairs={{0,2},{1,3},{2,0},{3,1},{4,6},{5,7},{6,4},{7,5},{8,10},{9,11},{10,... | collective-permute-start | bytes 983048 | tf_op jit(solution)/shard_map/ppermute | solution.py:120
  262.0 32.4 %collective-permute-start.52 = (bf16[4,64,640]{2,1,0:T(8,128)(2,1)}, bf16[4,64,640]{2,1,0:T(8,128)(2,1)}, u32[]{:S(2)}, u32[]{:S(2)}) collective-permute-start(bf16[4,64,640]{2,1,0:T(8,128)(2,1)} %add_convert_fusion.1), channel_id=1, source_target_pairs={{0,2},{1,3},{2,0},{3,1},{4,6},{5,7},{6,4},{7,5},{8,10},{9,11},{10,... | collective-permute-start | bytes 983048 | tf_op jit(solution)/shard_map/ppermute | solution.py:120
  328.0 31.5 %collective-permute-start.57 = (bf16[8,48,512]{2,1,0:T(8,128)(2,1)S(1)}, bf16[8,48,512]{2,1,0:T(8,128)(2,1)S(1)}, u32[]{:S(2)}, u32[]{:S(2)}) collective-permute-start(bf16[8,48,512]{2,1,0:T(8,128)(2,1)S(1)} %get-tuple-element.84), channel_id=1, source_target_pairs={{0,1},{1,0},{2,3},{3,2},{4,5},{5,4},{6,7},{7,6},{8,9},{9,8},{10,11... | collective-permute-start | bytes 1179656 | tf_op jit(solution)/shard_map/ppermute | solution.py:124
  329.3 12.0 %collective-permute-start.55 = (bf16[40,1024]{1,0:T(8,128)(2,1)S(1)}, bf16[40,1024]{1,0:T(8,128)(2,1)S(1)}, u32[]{:S(2)}, u32[]{:S(2)}) collective-permute-start(bf16[40,1024]{1,0:T(8,128)(2,1)S(1)} %get-tuple-element.151), channel_id=1, source_target_pairs={{0,12},{1,13},{2,14},{3,15},{4,0},{5,1},{6,2},{7,3},{8,4},{9,5},{1... | collective-permute-start | bytes 245768 | tf_op jit(solution)/shard_map/ppermute | solution.py:108
  331.4 10.5 %collective-permute-start.54 = (bf16[40,1024]{1,0:T(8,128)(2,1)S(1)}, bf16[40,1024]{1,0:T(8,128)(2,1)S(1)}, u32[]{:S(2)}, u32[]{:S(2)}) collective-permute-start(bf16[40,1024]{1,0:T(8,128)(2,1)S(1)} %get-tuple-element.152), channel_id=1, source_target_pairs={{0,8},{1,9},{2,10},{3,11},{4,12},{5,13},{6,14},{7,15},{8,0},{9,1},... | collective-permute-start | bytes 245768 | tf_op jit(solution)/shard_map/ppermute | solution.py:108
  333.4 8.6 %collective-permute-start.53 = (bf16[40,1024]{1,0:T(8,128)(2,1)S(1)}, bf16[40,1024]{1,0:T(8,128)(2,1)S(1)}, u32[]{:S(2)}, u32[]{:S(2)}) collective-permute-start(bf16[40,1024]{1,0:T(8,128)(2,1)S(1)} %get-tuple-element.150), channel_id=1, source_target_pairs={{0,4},{1,5},{2,6},{3,7},{4,8},{5,9},{6,10},{7,11},{8,12},{9,13},{1... | collective-permute-start | bytes 245768 | tf_op jit(solution)/shard_map/ppermute | solution.py:108
  335.5 9.0 %collective-permute-start.65 = (bf16[64,640]{1,0:T(8,128)(2,1)S(1)}, bf16[64,640]{1,0:T(8,128)(2,1)S(1)}, u32[]{:S(2)}, u32[]{:S(2)}) collective-permute-start(bf16[64,640]{1,0:T(8,128)(2,1)S(1)} %get-tuple-element.148), channel_id=1, source_target_pairs={{0,12},{1,13},{2,14},{3,15},{4,0},{5,1},{6,2},{7,3},{8,4},{9,5},{1... | collective-permute-start | bytes 245768 | tf_op jit(solution)/shard_map/ppermute | solution.py:108
  341.3 7.3 %collective-permute-start.64 = (bf16[64,640]{1,0:T(8,128)(2,1)S(1)}, bf16[64,640]{1,0:T(8,128)(2,1)S(1)}, u32[]{:S(2)}, u32[]{:S(2)}) collective-permute-start(bf16[64,640]{1,0:T(8,128)(2,1)S(1)} %get-tuple-element.149), channel_id=1, source_target_pairs={{0,8},{1,9},{2,10},{3,11},{4,12},{5,13},{6,14},{7,15},{8,0},{9,1},... | collective-permute-start | bytes 245768 | tf_op jit(solution)/shard_map/ppermute | solution.py:108
  341.9 6.7 %collective-permute-start.63 = (bf16[64,640]{1,0:T(8,128)(2,1)S(1)}, bf16[64,640]{1,0:T(8,128)(2,1)S(1)}, u32[]{:S(2)}, u32[]{:S(2)}) collective-permute-start(bf16[64,640]{1,0:T(8,128)(2,1)S(1)} %get-tuple-element.147), channel_id=1, source_target_pairs={{0,4},{1,5},{2,6},{3,7},{4,8},{5,9},{6,10},{7,11},{8,12},{9,13},{1... | collective-permute-start | bytes 245768 | tf_op jit(solution)/shard_map/ppermute | solution.py:108
  342.0 18.3 %collective-permute-start.67 = (bf16[64,4096]{1,0:T(8,128)(2,1)S(1)}, bf16[64,4096]{1,0:T(8,128)(2,1)S(1)}, u32[]{:S(2)}, u32[]{:S(2)}) collective-permute-start(bf16[64,4096]{1,0:T(8,128)(2,1)S(1)} %bitcast.164), channel_id=1, source_target_pairs={{0,16},{16,0},{1,17},{17,1},{2,18},{18,2},{3,19},{19,3},{4,20},{20... | collective-permute-start | bytes 1572872 | tf_op jit(solution)/shard_map/ppermute | solution.py:171
  344.5 13.3 %collective-permute-start.56 = (bf16[40,1024]{1,0:T(8,128)(2,1)S(1)}, bf16[40,1024]{1,0:T(8,128)(2,1)S(1)}, u32[]{:S(2)}, u32[]{:S(2)}) collective-permute-start(bf16[40,1024]{1,0:T(8,128)(2,1)S(1)} %fusion.124), channel_id=1, source_target_pairs={{0,16},{16,0},{1,17},{17,1},{2,18},{18,2},{3,19},{19,3},{4,20},{20... | collective-permute-start | bytes 245768 | tf_op jit(solution)/shard_map/ppermute | solution.py:171
  349.6 9.0 %collective-permute-start.66 = (bf16[64,640]{1,0:T(8,128)(2,1)S(1)}, bf16[64,640]{1,0:T(8,128)(2,1)S(1)}, u32[]{:S(2)}, u32[]{:S(2)}) collective-permute-start(bf16[64,640]{1,0:T(8,128)(2,1)S(1)} %fusion.121), channel_id=1, source_target_pairs={{0,16},{16,0},{1,17},{17,1},{2,18},{18,2},{3,19},{19,3},{4,20},{20... | collective-permute-start | bytes 245768 | tf_op jit(solution)/shard_map/ppermute | solution.py:171
  359.6 5.7 %collective-permute-start.58 = (bf16[4,48,512]{2,1,0:T(8,128)(2,1)S(1)}, bf16[4,48,512]{2,1,0:T(8,128)(2,1)S(1)}, u32[]{:S(2)}, u32[]{:S(2)}) collective-permute-start(bf16[4,48,512]{2,1,0:T(8,128)(2,1)S(1)} %add_convert_fusion.3), channel_id=1, source_target_pairs={{0,2},{1,3},{2,0},{3,1},{4,6},{5,7},{6,4},{7,5},{8,10},{9,11},{10,... | collective-permute-start | bytes 589832 | tf_op jit(solution)/shard_map/ppermute | solution.py:120
  365.4 6.6 %collective-permute-start.61 = (bf16[48,512]{1,0:T(8,128)(2,1)S(1)}, bf16[48,512]{1,0:T(8,128)(2,1)S(1)}, u32[]{:S(2)}, u32[]{:S(2)}) collective-permute-start(bf16[48,512]{1,0:T(8,128)(2,1)S(1)} %get-tuple-element.158), channel_id=1, source_target_pairs={{0,12},{1,13},{2,14},{3,15},{4,0},{5,1},{6,2},{7,3},{8,4},{9,5},{1... | collective-permute-start | bytes 147464 | tf_op jit(solution)/shard_map/ppermute | solution.py:108
  368.9 5.0 %collective-permute-start.60 = (bf16[48,512]{1,0:T(8,128)(2,1)S(1)}, bf16[48,512]{1,0:T(8,128)(2,1)S(1)}, u32[]{:S(2)}, u32[]{:S(2)}) collective-permute-start(bf16[48,512]{1,0:T(8,128)(2,1)S(1)} %get-tuple-element.159), channel_id=1, source_target_pairs={{0,8},{1,9},{2,10},{3,11},{4,12},{5,13},{6,14},{7,15},{8,0},{9,1},... | collective-permute-start | bytes 147464 | tf_op jit(solution)/shard_map/ppermute | solution.py:108
  369.3 5.9 %collective-permute-start.59 = (bf16[48,512]{1,0:T(8,128)(2,1)S(1)}, bf16[48,512]{1,0:T(8,128)(2,1)S(1)}, u32[]{:S(2)}, u32[]{:S(2)}) collective-permute-start(bf16[48,512]{1,0:T(8,128)(2,1)S(1)} %get-tuple-element.157), channel_id=1, source_target_pairs={{0,4},{1,5},{2,6},{3,7},{4,8},{5,9},{6,10},{7,11},{8,12},{9,13},{1... | collective-permute-start | bytes 147464 | tf_op jit(solution)/shard_map/ppermute | solution.py:108
  375.2 4.2 %collective-permute-start.62 = (bf16[48,512]{1,0:T(8,128)(2,1)S(1)}, bf16[48,512]{1,0:T(8,128)(2,1)S(1)}, u32[]{:S(2)}, u32[]{:S(2)}) collective-permute-start(bf16[48,512]{1,0:T(8,128)(2,1)S(1)} %fusion.135), channel_id=1, source_target_pairs={{0,16},{16,0},{1,17},{17,1},{2,18},{18,2},{3,19},{19,3},{4,20},{20... | collective-permute-start | bytes 147464 | tf_op jit(solution)/shard_map/ppermute | solution.py:171
  (85 other events, 758.1 us)
Sparse Core Ops, SparseCore 0:
  11.4 104.8 all-gather.2
  180.0 137.4 reduce-scatter.1
where the time goes:
time: 394 us; the launch traced here: 388 us
  waiting for transfers between devices  155 us (39%)
  starting transfers between devices  82 us (21%)
  other arithmetic  57.7 us (15%)
  Pallas kernels  43.6 us (11%)
  local copies, waits for them, and re-layouts  20.8 us (5%)
  between operations  16.1 us (4%)
  matrix products  12.9 us (3%)
    ppermute x17, waiting for transfers between devices, swap_x(): return lax.ppermute(values, 'group', [(i, i ^ 2) for i in range(MEMBERS)])  76.7 us
    ppermute x15, starting transfers between devices, shift_z(): lax.ppermute(values, 'group', [(i, (i + 4 * k) % MEMBERS) for i in range(...  35.5 us
    ppermute x17, starting transfers between devices, swap_x(): return lax.ppermute(values, 'group', [(i, i ^ 2) for i in range(MEMBERS)])  30 us
    reduce_scatter x1, waiting for transfers between devices, per_device(): mine = lax.psum_scatter(packed, 'group', scatter_dimension=0, tiled=False)  23.1 us
    pallas_call x1, Pallas kernels, feed_back(): pl.pallas_call(feed_back_kernel, out_shape=(jax.ShapeDtypeStruct((tokens_...  20.6 us
    ppermute x2, waiting for transfers between devices, line_down(): lax.ppermute(values, 'group', [(i, i - 4) for i in range(4 * lowest, MEMB...  18 us
    unnamed x168, local copies, waits for them, and re-layouts  17.3 us
    ppermute x2, waiting for transfers between devices, line_up(): lax.ppermute(values, 'group', [(i, i + 4) for i in range(4 * lowest, MEMB...  15 us
  transfers between devices with their start and end apart: 70, of which 27 were waited for; matrix products, arithmetic and copies ran while one was open for 13% of the time, Pallas kernels for 5%

commit v1 on v0

--- a/solution.py
+++ b/solution.py
@@ -510,7 +510,7 @@
         copy.wait()
 
     def one_stream(stream, carry):
-        first, bound, low, _ = key_range(info, stream)
+        first, bound, low, high = key_range(info, stream)
         mine = pl.ds(pl.multiple_of(stream * SEG, SEG), SEG)
         for head in range(HQ):
             rows = slice(head * SEG, (head + 1) * SEG)
@@ -524,28 +524,47 @@
             both = grad.astype(F32) * o_ref[mine, lanes].astype(F32)
             delta[:, rows] = jnp.sum((both[:, 0:128] + both[:, 128:256]).T, axis=0, keepdims=True)
         dqt[...] = jnp.zeros_like(dqt)
-        shape = (SEG, HQ * SEG)
-
-        def visit(j, carry):
+
+        def visit(j, masked):
             keys = kv[j, stream, :, 0:HD]
             values = kv[j, stream, :, HD : 2 * HD]
-            score = jnp.dot(keys, qt[...], preferred_element_type=F32)
-            prob = jnp.exp2(score * (SCALE_SCORE * LOG2E) - lse_ref[stream])
-            row = first + (lax.broadcasted_iota(jnp.int32, (1, HQ * SEG), 1) & (SEG - 1))
-            start = jnp.where(row >= bound, bound, 0)
-            col = j * SEG + lax.broadcasted_iota(jnp.int32, shape, 0)
-            prob = jnp.where((col <= row) & (col >= start), prob, 0.0)
-            dprob = jnp.dot(values, dot_[...], preferred_element_type=F32)
-            dscore = (prob * (dprob - delta[...])).astype(BF16)
-            dv = jnp.dot(prob.astype(BF16), dos[...], preferred_element_type=F32)
-            dk = jnp.dot(dscore, qs[...], preferred_element_type=F32)
-            dqt[...] += jnp.dot(keys.T, dscore, preferred_element_type=F32)
+            width = HQ * SEG // 2
+            if masked:
+                row = first + (lax.broadcasted_iota(jnp.int32, (1, width), 1) & (SEG - 1))
+                start = jnp.where(row >= bound, bound, 0)
+                col = j * SEG + lax.broadcasted_iota(jnp.int32, (SEG, width), 0)
+                mask = (col <= row) & (col >= start)
+            keys_turned = keys.T
+            dks, dvs = [], []
+            for part in range(2):
+                at = slice(part * width, (part + 1) * width)
+                score = jnp.dot(keys, qt[:, at], preferred_element_type=F32)
+                dprob = jnp.dot(values, dot_[:, at], preferred_element_type=F32)
+                prob = jnp.exp2(score * (SCALE_SCORE * LOG2E) - lse_ref[stream, :, at])
+                if masked:
+                    prob = jnp.where(mask, prob, 0.0)
+                dscore = (prob * (dprob - delta[:, at])).astype(BF16)
+                dvs.append(jnp.dot(prob.astype(BF16), dos[at], preferred_element_type=F32))
+                dks.append(jnp.dot(dscore, qs[at], preferred_element_type=F32))
+                dqt[:, at] += jnp.dot(keys_turned, dscore, preferred_element_type=F32)
             place = ((j & 1) ^ c) * (2 * REACH) + (z - (j >> 2)) * 2 + (((j >> 1) & 1) ^ x)
-            dkv[place, stream, :, 0:HD] = (dk * SCALE_SCORE).astype(BF16)
-            dkv[place, stream, :, HD : 2 * HD] = dv.astype(BF16)
+            dkv[place, stream, :, 0:HD] = ((dks[0] + dks[1]) * SCALE_SCORE).astype(BF16)
+            dkv[place, stream, :, HD : 2 * HD] = (dvs[0] + dvs[1]).astype(BF16)
+
+        begin = low // SEG
+        diagonal = first // SEG
+        clear = jnp.clip((high + SEG - 1) // SEG, begin, diagonal)
+
+        def masked_step(i, carry):
+            visit(jnp.where(i < clear, i, diagonal), True)
             return carry
 
-        lax.fori_loop(low // SEG, first // SEG + 1, visit, 0)
+        def clear_step(j, carry):
+            visit(j, False)
+            return carry
+
+        lax.fori_loop(begin, clear + 1, masked_step, 0)
+        lax.fori_loop(clear, diagonal, clear_step, 0)
         for head in range(HQ):
             rows = slice(head * SEG, (head + 1) * SEG)
             dq_ref[mine, head * HD : (head + 1) * HD] = dqt[:, rows].T * SCALE_SCORE
@@ -593,7 +612,7 @@
         ],
         compiler_params=pltpu.CompilerParams(vmem_limit_bytes=52 * 1024 * 1024),
         cost_estimate=pl.CostEstimate(
-            flops=17_000_000_000, bytes_accessed=20_000_000, transcendentals=7_000_000
+            flops=500_000_000, bytes_accessed=1_000_000, transcendentals=0
         ),
         name="attention_backward",
     )(info, query, out, grad_out, lse, *blocks)
@@ -719,9 +738,11 @@
     )
     came_q = swap_core(far_q)
     over_q = scatter_x(near_q, came_q)
-    grad_kv, over_q, over_out, mine = lax.optimization_barrier((grad_kv, over_q, over_out, mine))
-    sum_out = over_replicas(scatter_z(near_out, came_out, over_out))
-    sum_q = over_replicas(scatter_z(near_q, came_q, over_q))
+    shard_q = scatter_z(near_q, came_q, over_q)
+    shard_out = scatter_z(near_out, came_out, over_out)
+    grad_kv, shard_q, shard_out, mine = lax.optimization_barrier(
+        (grad_kv, shard_q, shard_out, mine)
+    )
     grad_key_rows, grad_gain_k = pull_key(grad_kv[:, :HD])
     kv_grad_low = jnp.concatenate(
         [grad_key_rows.astype(BF16), grad_kv[:, HD:].astype(BF16)], axis=1
@@ -741,7 +762,12 @@
         info, [(input_low, kv_grad_low)], gains_out, 2 * HD, "gradient_kv"
     )
     came_kv = swap_core(far_kv)
-    sum_kv = over_replicas(scatter_z(near_kv, came_kv, scatter_x(near_kv, came_kv)))
+    over_kv, mine, shard_q, shard_out = lax.optimization_barrier(
+        (scatter_x(near_kv, came_kv), mine, shard_q, shard_out)
+    )
+    sum_kv = over_replicas(scatter_z(near_kv, came_kv, over_kv))
+    sum_q = over_replicas(shard_q)
+    sum_out = over_replicas(shard_out)
     shard_qkv = jnp.concatenate([sum_q, sum_kv[:-8]], axis=1)
     shard_gains = sum_kv[-1, :gain_count]
     sum_packed = over_replicas(mine)

time: 394 us -> 390 us (0.990)
  starting transfers between devices: 82 us -> 124 us
  waiting for transfers between devices: 155 us -> 115 us
  other arithmetic: 57.7 us -> 50.8 us
    ppermute x15, starting transfers between devices: 35.5 us -> 72.3 us  [shift_z(): lax.ppermute(values, 'group', [(i, (i + 4 * k) % MEMBERS) for i in range(...]
    reduce_scatter x1, waiting for transfers between devices: 23.1 us -> 0.02 us  [per_device(): mine = lax.psum_scatter(packed, 'group', scatter_dimension=0, tiled=False)]
    ppermute x2, waiting for transfers between devices: 18 us -> 0.01 us  [line_down(): lax.ppermute(values, 'group', [(i, i - 4) for i in range(4 * lowest, MEMB...]
    ppermute x17, waiting for transfers between devices: 76.7 us -> 63.2 us  [swap_x(): return lax.ppermute(values, 'group', [(i, i ^ 2) for i in range(MEMBERS)])]
    ppermute x15, waiting for transfers between devices: 10.8 us -> 22.2 us  [shift_z(): lax.ppermute(values, 'group', [(i, (i + 4 * k) % MEMBERS) for i in range(...]
    ppermute x17, starting transfers between devices: 30 us -> 34.2 us  [swap_x(): return lax.ppermute(values, 'group', [(i, i ^ 2) for i in range(MEMBERS)])]
    ppermute x4, waiting for transfers between devices: 8.88 us -> 12.9 us  [over_replicas(): other = lax.ppermute(shard, 'replica', [(0, 1), (1, 0)])]
    unnamed x168 -> x200, local copies, waits for them, and re-layouts: 17.3 us -> 18.6 us
  transfers between devices with their start and end apart: 70 -> 70, of which waited for: 27 -> 21; matrix products, arithmetic and copies ran while one was open for 13% -> 11% of each run, Pallas kernels for 5% -> 6%
where the time goes in v1:
time: 390 us; the launch traced here: 384 us
  starting transfers between devices  124 us (32%)
  waiting for transfers between devices  115 us (29%)
  other arithmetic  50.8 us (13%)
  Pallas kernels  44.2 us (11%)
  local copies, waits for them, and re-layouts  20.2 us (5%)
  between operations  16.4 us (4%)
  matrix products  12.9 us (3%)
    ppermute x15, starting transfers between devices, shift_z(): lax.ppermute(values, 'group', [(i, (i + 4 * k) % MEMBERS) for i in range(...  72.3 us
    ppermute x17, waiting for transfers between devices, swap_x(): return lax.ppermute(values, 'group', [(i, i ^ 2) for i in range(MEMBERS)])  63.2 us
    ppermute x17, starting transfers between devices, swap_x(): return lax.ppermute(values, 'group', [(i, i ^ 2) for i in range(MEMBERS)])  34.2 us
    ppermute x15, waiting for transfers between devices, shift_z(): lax.ppermute(values, 'group', [(i, (i + 4 * k) % MEMBERS) for i in range(...  22.2 us
    pallas_call x1, Pallas kernels, feed_back(): pl.pallas_call(feed_back_kernel, out_shape=(jax.ShapeDtypeStruct((tokens_...  20.5 us
    unnamed x200, local copies, waits for them, and re-layouts  18.6 us
    ppermute x2, waiting for transfers between devices, line_up(): lax.ppermute(values, 'group', [(i, i + 4) for i in range(4 * lowest, MEMB...  14.8 us
    ppermute x4, waiting for transfers between devices, over_replicas(): other = lax.ppermute(shard, 'replica', [(0, 1), (1, 0)])  12.9 us
  transfers between devices with their start and end apart: 70, of which 21 were waited for; matrix products, arithmetic and copies ran while one was open for 11% of the time, Pallas kernels for 6%

profile of v1, /device:TPU:0, one launch (start us, length us, event | category | flops | bytes accessed | tf_op | source)
XLA Modules:
  0.0 383.8 jit_solution(4064375119898519278)
XLA Ops:
  11.4 3.1 collective-permute-start
  14.5 2.6 collective-permute-start.1
  17.0 1.3 collective-permute-start.2
  18.4 1.5 collective-permute-start.3
  21.2 1.6 collective-permute-start.5
  24.9 2.2 collective-permute-done.5.refs_6_
  27.1 1.7 collective-permute-done.6.refs_7_
  34.6 1.7 collective-permute-start.15
  36.3 2.1 collective-permute-start.17
  38.5 14.8 %collective-permute-done.15.refs_1_ = bf16[2,256,512]{2,1,0:T(8,128)(2,1)S(1)} collective-permute-done((bf16[2,256,512]{2,1,0:T(8,128)(2,1)S(1)}, bf16[2,256,512]{2,1,0:T(8,128)(2,1)S(1)}, u32[]{:S(2)}, u32[]{:S(2)}) %collective-permute-start.15) | collective-permute-done | bytes 524320 | tf_op jit(solution)/shard_map/ppermute | solution.py:112
  53.9 2.0 collective-permute-start.18
  55.9 23.6 %collective-permute-done.18.refs_4_ = bf16[2,256,512]{2,1,0:T(8,128)(2,1)S(1)} collective-permute-done((bf16[2,256,512]{2,1,0:T(8,128)(2,1)S(1)}, bf16[2,256,512]{2,1,0:T(8,128)(2,1)S(1)}, u32[]{:S(2)}, u32[]{:S(2)}) %collective-permute-start.18) | collective-permute-done | bytes 524320 | tf_op jit(solution)/shard_map/ppermute | solution.py:120
  79.5 9.9 %collective-permute-start.19 = (bf16[40,1024]{1,0:T(8,128)(2,1)S(1)}, bf16[40,1024]{1,0:T(8,128)(2,1)S(1)}, u32[]{:S(2)}, u32[]{:S(2)}) collective-permute-start(bf16[40,1024]{1,0:T(8,128)(2,1)S(1)} %slice.352.refs_0_), channel_id=1, source_target_pairs={{0,4},{1,5},{2,6},{3,7},{4,8},{5,9},{6,10},{7,11},{8,12},{9,13},{1... | collective-permute-start | bytes 245768 | tf_op jit(solution)/shard_map/ppermute | solution.py:108
  89.4 2.9 collective-permute-start.20
  92.3 2.6 collective-permute-start.21
  94.9 3.0 collective-permute-start.22
  97.9 2.1 collective-permute-start.23
  100.0 1.6 collective-permute-done.20.refs_2_
  101.6 4.1 %collective-permute-start.24 = (bf16[40,1024]{1,0:T(8,128)(2,1)S(1)}, bf16[40,1024]{1,0:T(8,128)(2,1)S(1)}, u32[]{:S(2)}, u32[]{:S(2)}) collective-permute-start(bf16[40,1024]{1,0:T(8,128)(2,1)S(1)} %collective-permute-done.20.refs_2_), channel_id=1, source_target_pairs={{0,2},{1,3},{2,0},{3,1},{4,6},{5,7},{6,4},{7,5},{8,10},{9,11},{10,... | collective-permute-start | bytes 245768 | tf_op jit(solution)/shard_map/ppermute | solution.py:120
  106.4 2.0 collective-permute-done.24.refs_6_
  108.4 1.8 collective-permute-done.25.refs_7_
  116.1 1.6 fusion.132
  122.5 3.0 collective-permute-done.34.refs_5_
  129.2 4.0 %attention_forward.1 = (bf16[512,1024]{1,0:T(8,128)(2,1)S(1)}, f32[2,1,1024]{2,1,0:T(1,128)S(1)}) custom-call(s32[6]{0:T(128)S(1)} %concatenate.42.info.refs_0_, bf16[512,1024]{1,0:T(8,128)(2,1)S(1)} %fusion.125.q_ref, bf16[2,256,512]{2,1,0:T(8,128)(2,1)S(1)} %bitcast.160, bf16[2,256,512]{2,1,0:T(8,128)(2,1)S(1)} %collective-permute-done.15.refs_1_, ...), custom_call_target="tpu_custom_call" | custom-call | flops 7000000000 | bytes 9000000 | tf_op jit(solution)/shard_map/attention_forward/pallas_call | solution.py:471
  138.2 3.7 copy-done
  145.7 3.4 fusion.166.gate_up
  149.2 1.7 fusion.8.hidden
  150.8 1.7 copy-done.30
  152.5 1.9 multiply_reduce_fusion.4
  155.5 1.6 fusion.12
  157.1 20.5 %feed_back.1 = (f32[512,640]{1,0:T(8,128)}, bf16[16,64,4096]{2,1,0:T(8,128)(2,1)}) custom-call(bf16[512,640]{1,0:T(8,128)(2,1)} %get-tuple-element.161.down, bf16[512,2048]{1,0:T(8,128)(2,1)} %copy-done.48, f32[512,4096]{1,0:T(8,128)} %copy-done.30, bf16[512,640]{1,0:T(8,128)(2,1)} %copy-done.45, bf16[2048,640]{1,0:T(8,128)(2,1)} %copy-done.25, ...), custom_call_target="tpu_custom_call" | custom-call | flops 10737418240 | bytes 32000000 | tf_op jit(solution)/shard_map/feed_back/pallas_call | solution.py:376
  177.6 2.8 multiply_reduce_fusion
  180.5 2.7 multiply_reduce_fusion.1
  184.6 1.7 gradient_out.1
  186.3 2.0 convolution_convert_fusion.do_ref
  188.4 12.2 %attention_backward.1 = (f32[512,1024]{1,0:T(8,128)}, bf16[2,2,256,512]{3,2,1,0:T(8,128)(2,1)}, bf16[2,2,256,512]{3,2,1,0:T(8,128)(2,1)}, bf16[2,2,256,512]{3,2,...) custom-call(s32[6]{0:T(128)S(1)} %concatenate.42.info.refs_0_, ...), custom_call_target="tpu_custom_call" | custom-call | flops 500000000 | bytes 1000000 | tf_op jit(solution)/shard_map/attention_backward/pallas_call | solution.py:594
  200.6 2.7 collective-permute-start.43
  203.4 3.0 fusion.107
  210.1 2.3 gradient_q.1
  213.4 1.5 convert_element_type.461
  215.1 6.9 %collective-permute-start.46 = (bf16[2,256,512]{2,1,0:T(8,128)(2,1)S(1)}, bf16[2,256,512]{2,1,0:T(8,128)(2,1)S(1)}, u32[]{:S(2)}, u32[]{:S(2)}) collective-permute-start(bf16[2,256,512]{2,1,0:T(8,128)(2,1)S(1)} %fusion.24), channel_id=1, source_target_pairs={{0,2},{1,3},{2,0},{3,1},{4,6},{5,7},{6,4},{7,5},{8,10},{9,11},{10,... | collective-permute-start | bytes 1572872 | tf_op jit(solution)/shard_map/ppermute | solution.py:120
  223.3 1.6 convert_element_type.456
  225.1 2.0 collective-permute-start.44
  227.1 18.2 %collective-permute-done.46 = bf16[2,256,512]{2,1,0:T(8,128)(2,1)S(1)} collective-permute-done((bf16[2,256,512]{2,1,0:T(8,128)(2,1)S(1)}, bf16[2,256,512]{2,1,0:T(8,128)(2,1)S(1)}, u32[]{:S(2)}, u32[]{:S(2)}) %collective-permute-start.46) | collective-permute-done | bytes 524320 | tf_op jit(solution)/shard_map/ppermute | solution.py:120
  246.3 2.0 collective-permute-start.55
  248.3 4.6 %collective-permute-done.50 = bf16[4,40,1024]{2,1,0:T(8,128)(2,1)S(1)} collective-permute-done((bf16[4,40,1024]{2,1,0:T(8,128)(2,1)S(1)}, bf16[4,40,1024]{2,1,0:T(8,128)(2,1)S(1)}, u32[]{:S(2)}, u32[]{:S(2)}) %collective-permute-start.50) | collective-permute-done | bytes 327712 | tf_op jit(solution)/shard_map/ppermute | solution.py:120
  254.0 28.6 %collective-permute-start.53 = (bf16[40,1024]{1,0:T(8,128)(2,1)S(1)}, bf16[40,1024]{1,0:T(8,128)(2,1)S(1)}, u32[]{:S(2)}, u32[]{:S(2)}) collective-permute-start(bf16[40,1024]{1,0:T(8,128)(2,1)S(1)} %get-tuple-element.159), channel_id=1, source_target_pairs={{0,12},{1,13},{2,14},{3,15},{4,0},{5,1},{6,2},{7,3},{8,4},{9,5},{1... | collective-permute-start | bytes 245768 | tf_op jit(solution)/shard_map/ppermute | solution.py:108
  284.3 2.1 collective-permute-start.42
  286.7 1.4 collective-permute-start.48
  288.2 18.2 %collective-permute-start.58 = (bf16[64,640]{1,0:T(8,128)(2,1)S(1)}, bf16[64,640]{1,0:T(8,128)(2,1)S(1)}, u32[]{:S(2)}, u32[]{:S(2)}) collective-permute-start(bf16[64,640]{1,0:T(8,128)(2,1)S(1)} %get-tuple-element.156), channel_id=1, source_target_pairs={{0,12},{1,13},{2,14},{3,15},{4,0},{5,1},{6,2},{7,3},{8,4},{9,5},{1... | collective-permute-start | bytes 245768 | tf_op jit(solution)/shard_map/ppermute | solution.py:108
  307.1 1.6 fusion.124
  308.7 12.5 %collective-permute-done.58 = bf16[64,640]{1,0:T(8,128)(2,1)S(1)} collective-permute-done((bf16[64,640]{1,0:T(8,128)(2,1)S(1)}, bf16[64,640]{1,0:T(8,128)(2,1)S(1)}, u32[]{:S(2)}, u32[]{:S(2)}) %collective-permute-start.58) | collective-permute-done | bytes 81952 | tf_op jit(solution)/shard_map/ppermute | solution.py:108
  321.3 5.6 %collective-permute-done.57 = bf16[64,640]{1,0:T(8,128)(2,1)S(1)} collective-permute-done((bf16[64,640]{1,0:T(8,128)(2,1)S(1)}, bf16[64,640]{1,0:T(8,128)(2,1)S(1)}, u32[]{:S(2)}, u32[]{:S(2)}) %collective-permute-start.57) | collective-permute-done | bytes 81952 | tf_op jit(solution)/shard_map/ppermute | solution.py:108
  326.8 2.4 collective-permute-done.56
  333.2 2.3 fusion.19
  337.0 1.7 collective-permute-done.59
  338.8 2.0 collective-permute-start.60
  340.8 5.2 %collective-permute-done.60 = bf16[4,48,512]{2,1,0:T(8,128)(2,1)S(1)} collective-permute-done((bf16[4,48,512]{2,1,0:T(8,128)(2,1)S(1)}, bf16[4,48,512]{2,1,0:T(8,128)(2,1)S(1)}, u32[]{:S(2)}, u32[]{:S(2)}) %collective-permute-start.60) | collective-permute-done | bytes 196640 | tf_op jit(solution)/shard_map/ppermute | solution.py:120
  348.2 3.0 fusion.14
  351.3 3.5 collective-permute-start.61
  354.8 1.9 collective-permute-start.67
  357.0 3.1 collective-permute-done.66
  361.0 9.7 %collective-permute-done.65 = bf16[48,512]{1,0:T(8,128)(2,1)S(1)} collective-permute-done((bf16[48,512]{1,0:T(8,128)(2,1)S(1)}, bf16[48,512]{1,0:T(8,128)(2,1)S(1)}, u32[]{:S(2)}, u32[]{:S(2)}) %collective-permute-start.65) | collective-permute-done | bytes 49184 | tf_op jit(solution)/shard_map/ppermute | solution.py:171
  373.9 1.5 divide_subtract_fusion
  (412 shorter events, 63.3 us)
Async XLA Ops:
  7.2 131.0 %all-gather.3.cloned.1.call-start = ((), (), s32[]{:S(2)}) async-start(), calls=%async_computation.2 | async-start | bytes 10027008 | tf_op jit(solution)/shard_map/all_gather | solution.py:669
  11.2 318.5 %reduce-scatter.2.cloned.1.call-start = ((), (), s32[]{:S(2)}) async-start(), calls=%async_computation.1 | async-start | bytes 8912896 | tf_op jit(solution)/shard_map/reduce_scatter | solution.py:716
  11.4 9.0 %collective-permute-start = (bf16[41,512]{1,0:T(8,128)(2,1)S(1)}, bf16[41,512]{1,0:T(8,128)(2,1)S(1)}, u32[]{:S(2)}, u32[]{:S(2)}) collective-permute-start(bf16[41,512]{1,0:T(8,128)(2,1)S(1)} %pad_maximum_fusion.5.refs_0_), channel_id=1, source_target_pairs={{0,4},{1,5},{2,6},{3,7},{4,8},{5,9},{6,10},{7,11},{8,12},{9,13},{1... | collective-permute-start | bytes 125960 | tf_op jit(solution)/shard_map/ppermute | solution.py:108
  14.5 6.5 %collective-permute-start.1 = (bf16[41,512]{1,0:T(8,128)(2,1)S(1)}, bf16[41,512]{1,0:T(8,128)(2,1)S(1)}, u32[]{:S(2)}, u32[]{:S(2)}) collective-permute-start(bf16[41,512]{1,0:T(8,128)(2,1)S(1)} %pad_maximum_fusion.5.refs_0_), channel_id=1, source_target_pairs={{0,8},{1,9},{2,10},{3,11},{4,12},{5,13},{6,14},{7,15},{8,0},{9,1},... | collective-permute-start | bytes 125960 | tf_op jit(solution)/shard_map/ppermute | solution.py:108
  17.0 4.1 %collective-permute-start.2 = (bf16[41,512]{1,0:T(8,128)(2,1)S(1)}, bf16[41,512]{1,0:T(8,128)(2,1)S(1)}, u32[]{:S(2)}, u32[]{:S(2)}) collective-permute-start(bf16[41,512]{1,0:T(8,128)(2,1)S(1)} %pad_maximum_fusion.5.refs_0_), channel_id=1, source_target_pairs={{0,12},{1,13},{2,14},{3,15},{4,0},{5,1},{6,2},{7,3},{8,4},{9,5},{1... | collective-permute-start | bytes 125960 | tf_op jit(solution)/shard_map/ppermute | solution.py:108
  18.4 4.4 %collective-permute-start.3 = (bf16[41,512]{1,0:T(8,128)(2,1)S(1)}, bf16[41,512]{1,0:T(8,128)(2,1)S(1)}, u32[]{:S(2)}, u32[]{:S(2)}) collective-permute-start(bf16[41,512]{1,0:T(8,128)(2,1)S(1)} %pad_maximum_fusion.5.refs_0_), channel_id=1, source_target_pairs={{0,2},{1,3},{2,0},{3,1},{4,6},{5,7},{6,4},{7,5},{8,10},{9,11},{10,... | collective-permute-start | bytes 125960 | tf_op jit(solution)/shard_map/ppermute | solution.py:120
  19.9 2.9 collective-permute-start.7
  20.3 4.6 %collective-permute-start.4 = (bf16[41,512]{1,0:T(8,128)(2,1)S(1)}, bf16[41,512]{1,0:T(8,128)(2,1)S(1)}, u32[]{:S(2)}, u32[]{:S(2)}) collective-permute-start(bf16[41,512]{1,0:T(8,128)(2,1)S(1)} %collective-permute-done.refs_1_), channel_id=1, source_target_pairs={{0,2},{1,3},{2,0},{3,1},{4,6},{5,7},{6,4},{7,5},{8,10},{9,11},{10,... | collective-permute-start | bytes 125960 | tf_op jit(solution)/shard_map/ppermute | solution.py:120
  20.9 7.8 %collective-permute-start.8 = (bf16[41,512]{1,0:T(8,128)(2,1)S(1)}, bf16[41,512]{1,0:T(8,128)(2,1)S(1)}, u32[]{:S(2)}, u32[]{:S(2)}) collective-permute-start(bf16[41,512]{1,0:T(8,128)(2,1)S(1)} %collective-permute-done.refs_1_), channel_id=1, source_target_pairs={{0,1},{1,0},{2,3},{3,2},{4,5},{5,4},{6,7},{7,6},{8,9},{9,8},{10,11... | collective-permute-start | bytes 125960 | tf_op jit(solution)/shard_map/ppermute | solution.py:124
  21.2 5.9 %collective-permute-start.5 = (bf16[41,512]{1,0:T(8,128)(2,1)S(1)}, bf16[41,512]{1,0:T(8,128)(2,1)S(1)}, u32[]{:S(2)}, u32[]{:S(2)}) collective-permute-start(bf16[41,512]{1,0:T(8,128)(2,1)S(1)} %collective-permute-done.1.refs_2_), channel_id=1, source_target_pairs={{0,2},{1,3},{2,0},{3,1},{4,6},{5,7},{6,4},{7,5},{8,10},{9,11},{10,... | collective-permute-start | bytes 125960 | tf_op jit(solution)/shard_map/ppermute | solution.py:120
  22.8 6.5 %collective-permute-start.9 = (bf16[41,512]{1,0:T(8,128)(2,1)S(1)}, bf16[41,512]{1,0:T(8,128)(2,1)S(1)}, u32[]{:S(2)}, u32[]{:S(2)}) collective-permute-start(bf16[41,512]{1,0:T(8,128)(2,1)S(1)} %collective-permute-done.1.refs_2_), channel_id=1, source_target_pairs={{0,1},{1,0},{2,3},{3,2},{4,5},{5,4},{6,7},{7,6},{8,9},{9,8},{10,11... | collective-permute-start | bytes 125960 | tf_op jit(solution)/shard_map/ppermute | solution.py:124
  22.8 6.0 %collective-permute-start.6 = (bf16[41,512]{1,0:T(8,128)(2,1)S(1)}, bf16[41,512]{1,0:T(8,128)(2,1)S(1)}, u32[]{:S(2)}, u32[]{:S(2)}) collective-permute-start(bf16[41,512]{1,0:T(8,128)(2,1)S(1)} %collective-permute-done.2.refs_3_), channel_id=1, source_target_pairs={{0,2},{1,3},{2,0},{3,1},{4,6},{5,7},{6,4},{7,5},{8,10},{9,11},{10,... | collective-permute-start | bytes 125960 | tf_op jit(solution)/shard_map/ppermute | solution.py:120
  24.9 5.1 %collective-permute-start.10 = (bf16[41,512]{1,0:T(8,128)(2,1)S(1)}, bf16[41,512]{1,0:T(8,128)(2,1)S(1)}, u32[]{:S(2)}, u32[]{:S(2)}) collective-permute-start(bf16[41,512]{1,0:T(8,128)(2,1)S(1)} %collective-permute-done.2.refs_3_), channel_id=1, source_target_pairs={{0,1},{1,0},{2,3},{3,2},{4,5},{5,4},{6,7},{7,6},{8,9},{9,8},{10,11... | collective-permute-start | bytes 125960 | tf_op jit(solution)/shard_map/ppermute | solution.py:124
  27.1 2.9 collective-permute-start.11
  34.6 18.6 %collective-permute-start.15 = (bf16[2,256,512]{2,1,0:T(8,128)(2,1)S(1)}, bf16[2,256,512]{2,1,0:T(8,128)(2,1)S(1)}, u32[]{:S(2)}, u32[]{:S(2)}) collective-permute-start(bf16[2,256,512]{2,1,0:T(8,128)(2,1)S(1)} %bitcast.157), channel_id=1, source_target_pairs={{0,4},{1,5},{2,6},{3,7},{4,8},{5,9},{6,10},{7,11},{8,12},{9,13},{1... | collective-permute-start | bytes 1572872 | tf_op jit(solution)/shard_map/ppermute | solution.py:112
  36.3 19.6 %collective-permute-start.17 = (bf16[2,256,512]{2,1,0:T(8,128)(2,1)S(1)}, bf16[2,256,512]{2,1,0:T(8,128)(2,1)S(1)}, u32[]{:S(2)}, u32[]{:S(2)}) collective-permute-start(bf16[2,256,512]{2,1,0:T(8,128)(2,1)S(1)} %bitcast.158), channel_id=1, source_target_pairs={{0,2},{1,3},{2,0},{3,1},{4,6},{5,7},{6,4},{7,5},{8,10},{9,11},{10,... | collective-permute-start | bytes 1572872 | tf_op jit(solution)/shard_map/ppermute | solution.py:120
  53.2 2.7 collective-permute-start.16
  53.9 25.6 %collective-permute-start.18 = (bf16[2,256,512]{2,1,0:T(8,128)(2,1)S(1)}, bf16[2,256,512]{2,1,0:T(8,128)(2,1)S(1)}, u32[]{:S(2)}, u32[]{:S(2)}) collective-permute-start(bf16[2,256,512]{2,1,0:T(8,128)(2,1)S(1)} %collective-permute-done.15.refs_1_), channel_id=1, source_target_pairs={{0,2},{1,3},{2,0},{3,1},{4,6},{5,7},{6,4},{7,5},{8,10},{9,11},{10,... | collective-permute-start | bytes 1572872 | tf_op jit(solution)/shard_map/ppermute | solution.py:120
  79.5 18.4 %collective-permute-start.19 = (bf16[40,1024]{1,0:T(8,128)(2,1)S(1)}, bf16[40,1024]{1,0:T(8,128)(2,1)S(1)}, u32[]{:S(2)}, u32[]{:S(2)}) collective-permute-start(bf16[40,1024]{1,0:T(8,128)(2,1)S(1)} %slice.352.refs_0_), channel_id=1, source_target_pairs={{0,4},{1,5},{2,6},{3,7},{4,8},{5,9},{6,10},{7,11},{8,12},{9,13},{1... | collective-permute-start | bytes 245768 | tf_op jit(solution)/shard_map/ppermute | solution.py:108
  89.4 12.2 %collective-permute-start.20 = (bf16[40,1024]{1,0:T(8,128)(2,1)S(1)}, bf16[40,1024]{1,0:T(8,128)(2,1)S(1)}, u32[]{:S(2)}, u32[]{:S(2)}) collective-permute-start(bf16[40,1024]{1,0:T(8,128)(2,1)S(1)} %slice.352.refs_0_), channel_id=1, source_target_pairs={{0,8},{1,9},{2,10},{3,11},{4,12},{5,13},{6,14},{7,15},{8,0},{9,1},... | collective-permute-start | bytes 245768 | tf_op jit(solution)/shard_map/ppermute | solution.py:108
  92.3 13.4 %collective-permute-start.21 = (bf16[40,1024]{1,0:T(8,128)(2,1)S(1)}, bf16[40,1024]{1,0:T(8,128)(2,1)S(1)}, u32[]{:S(2)}, u32[]{:S(2)}) collective-permute-start(bf16[40,1024]{1,0:T(8,128)(2,1)S(1)} %slice.352.refs_0_), channel_id=1, source_target_pairs={{0,12},{1,13},{2,14},{3,15},{4,0},{5,1},{6,2},{7,3},{8,4},{9,5},{1... | collective-permute-start | bytes 245768 | tf_op jit(solution)/shard_map/ppermute | solution.py:108
  94.9 10.8 %collective-permute-start.22 = (bf16[40,1024]{1,0:T(8,128)(2,1)S(1)}, bf16[40,1024]{1,0:T(8,128)(2,1)S(1)}, u32[]{:S(2)}, u32[]{:S(2)}) collective-permute-start(bf16[40,1024]{1,0:T(8,128)(2,1)S(1)} %slice.352.refs_0_), channel_id=1, source_target_pairs={{0,2},{1,3},{2,0},{3,1},{4,6},{5,7},{6,4},{7,5},{8,10},{9,11},{10,... | collective-permute-start | bytes 245768 | tf_op jit(solution)/shard_map/ppermute | solution.py:120
  97.9 7.9 %collective-permute-start.26 = (bf16[40,1024]{1,0:T(8,128)(2,1)S(1)}, bf16[40,1024]{1,0:T(8,128)(2,1)S(1)}, u32[]{:S(2)}, u32[]{:S(2)}) collective-permute-start(bf16[40,1024]{1,0:T(8,128)(2,1)S(1)} %slice.352.refs_0_), channel_id=1, source_target_pairs={{0,1},{1,0},{2,3},{3,2},{4,5},{5,4},{6,7},{7,6},{8,9},{9,8},{10,11... | collective-permute-start | bytes 245768 | tf_op jit(solution)/shard_map/ppermute | solution.py:124
  97.9 8.4 %collective-permute-start.23 = (bf16[40,1024]{1,0:T(8,128)(2,1)S(1)}, bf16[40,1024]{1,0:T(8,128)(2,1)S(1)}, u32[]{:S(2)}, u32[]{:S(2)}) collective-permute-start(bf16[40,1024]{1,0:T(8,128)(2,1)S(1)} %collective-permute-done.19.refs_1_), channel_id=1, source_target_pairs={{0,2},{1,3},{2,0},{3,1},{4,6},{5,7},{6,4},{7,5},{8,10},{9,11},{10,... | collective-permute-start | bytes 245768 | tf_op jit(solution)/shard_map/ppermute | solution.py:120
  101.6 6.8 %collective-permute-start.24 = (bf16[40,1024]{1,0:T(8,128)(2,1)S(1)}, bf16[40,1024]{1,0:T(8,128)(2,1)S(1)}, u32[]{:S(2)}, u32[]{:S(2)}) collective-permute-start(bf16[40,1024]{1,0:T(8,128)(2,1)S(1)} %collective-permute-done.20.refs_2_), channel_id=1, source_target_pairs={{0,2},{1,3},{2,0},{3,1},{4,6},{5,7},{6,4},{7,5},{8,10},{9,11},{10,... | collective-permute-start | bytes 245768 | tf_op jit(solution)/shard_map/ppermute | solution.py:120
  105.7 4.4 %collective-permute-start.25 = (bf16[40,1024]{1,0:T(8,128)(2,1)S(1)}, bf16[40,1024]{1,0:T(8,128)(2,1)S(1)}, u32[]{:S(2)}, u32[]{:S(2)}) collective-permute-start(bf16[40,1024]{1,0:T(8,128)(2,1)S(1)} %collective-permute-done.21.refs_3_), channel_id=1, source_target_pairs={{0,2},{1,3},{2,0},{3,1},{4,6},{5,7},{6,4},{7,5},{8,10},{9,11},{10,... | collective-permute-start | bytes 245768 | tf_op jit(solution)/shard_map/ppermute | solution.py:120
  105.8 4.4 %collective-permute-start.27 = (bf16[40,1024]{1,0:T(8,128)(2,1)S(1)}, bf16[40,1024]{1,0:T(8,128)(2,1)S(1)}, u32[]{:S(2)}, u32[]{:S(2)}) collective-permute-start(bf16[40,1024]{1,0:T(8,128)(2,1)S(1)} %collective-permute-done.19.refs_1_), channel_id=1, source_target_pairs={{0,1},{1,0},{2,3},{3,2},{4,5},{5,4},{6,7},{7,6},{8,9},{9,8},{10,11... | collective-permute-start | bytes 245768 | tf_op jit(solution)/shard_map/ppermute | solution.py:124
  105.8 4.9 %collective-permute-start.28 = (bf16[40,1024]{1,0:T(8,128)(2,1)S(1)}, bf16[40,1024]{1,0:T(8,128)(2,1)S(1)}, u32[]{:S(2)}, u32[]{:S(2)}) collective-permute-start(bf16[40,1024]{1,0:T(8,128)(2,1)S(1)} %collective-permute-done.20.refs_2_), channel_id=1, source_target_pairs={{0,1},{1,0},{2,3},{3,2},{4,5},{5,4},{6,7},{7,6},{8,9},{9,8},{10,11... | collective-permute-start | bytes 245768 | tf_op jit(solution)/shard_map/ppermute | solution.py:124
  106.3 4.4 %collective-permute-start.29 = (bf16[40,1024]{1,0:T(8,128)(2,1)S(1)}, bf16[40,1024]{1,0:T(8,128)(2,1)S(1)}, u32[]{:S(2)}, u32[]{:S(2)}) collective-permute-start(bf16[40,1024]{1,0:T(8,128)(2,1)S(1)} %collective-permute-done.21.refs_3_), channel_id=1, source_target_pairs={{0,1},{1,0},{2,3},{3,2},{4,5},{5,4},{6,7},{7,6},{8,9},{9,8},{10,11... | collective-permute-start | bytes 245768 | tf_op jit(solution)/shard_map/ppermute | solution.py:124
  108.4 2.8 collective-permute-start.30
  110.2 2.1 collective-permute-start.32
  110.8 11.6 %collective-permute-start.35 = (bf16[2,256,512]{2,1,0:T(8,128)(2,1)S(1)}, bf16[2,256,512]{2,1,0:T(8,128)(2,1)S(1)}, u32[]{:S(2)}, u32[]{:S(2)}) collective-permute-start(bf16[2,256,512]{2,1,0:T(8,128)(2,1)S(1)} %bitcast.159), channel_id=1, source_target_pairs={{0,1},{1,0},{2,3},{3,2},{4,5},{5,4},{6,7},{7,6},{8,9},{9,8},{10,11... | collective-permute-start | bytes 1572872 | tf_op jit(solution)/shard_map/ppermute | solution.py:124
  111.2 17.9 %collective-permute-start.36 = (bf16[2,256,512]{2,1,0:T(8,128)(2,1)S(1)}, bf16[2,256,512]{2,1,0:T(8,128)(2,1)S(1)}, u32[]{:S(2)}, u32[]{:S(2)}) collective-permute-start(bf16[2,256,512]{2,1,0:T(8,128)(2,1)S(1)} %collective-permute-done.15.refs_1_), channel_id=1, source_target_pairs={{0,1},{1,0},{2,3},{3,2},{4,5},{5,4},{6,7},{7,6},{8,9},{9,8},{10,11... | collective-permute-start | bytes 1572872 | tf_op jit(solution)/shard_map/ppermute | solution.py:124
  111.5 14.1 %collective-permute-start.34 = (bf16[2,256,512]{2,1,0:T(8,128)(2,1)S(1)}, bf16[2,256,512]{2,1,0:T(8,128)(2,1)S(1)}, u32[]{:S(2)}, u32[]{:S(2)}) collective-permute-start(bf16[2,256,512]{2,1,0:T(8,128)(2,1)S(1)} %collective-permute-done.16.refs_2_), channel_id=1, source_target_pairs={{0,2},{1,3},{2,0},{3,1},{4,6},{5,7},{6,4},{7,5},{8,10},{9,11},{10,... | collective-permute-start | bytes 1572872 | tf_op jit(solution)/shard_map/ppermute | solution.py:120
  112.3 16.8 %collective-permute-start.37 = (bf16[2,256,512]{2,1,0:T(8,128)(2,1)S(1)}, bf16[2,256,512]{2,1,0:T(8,128)(2,1)S(1)}, u32[]{:S(2)}, u32[]{:S(2)}) collective-permute-start(bf16[2,256,512]{2,1,0:T(8,128)(2,1)S(1)} %collective-permute-done.16.refs_2_), channel_id=1, source_target_pairs={{0,1},{1,0},{2,3},{3,2},{4,5},{5,4},{6,7},{7,6},{8,9},{9,8},{10,11... | collective-permute-start | bytes 1572872 | tf_op jit(solution)/shard_map/ppermute | solution.py:124
  112.3 16.8 %collective-permute-start.38 = (bf16[2,256,512]{2,1,0:T(8,128)(2,1)S(1)}, bf16[2,256,512]{2,1,0:T(8,128)(2,1)S(1)}, u32[]{:S(2)}, u32[]{:S(2)}) collective-permute-start(bf16[2,256,512]{2,1,0:T(8,128)(2,1)S(1)} %collective-permute-done.17.refs_3_), channel_id=1, source_target_pairs={{0,1},{1,0},{2,3},{3,2},{4,5},{5,4},{6,7},{7,6},{8,9},{9,8},{10,11... | collective-permute-start | bytes 1572872 | tf_op jit(solution)/shard_map/ppermute | solution.py:124
  122.4 6.7 %collective-permute-start.39 = (bf16[2,256,512]{2,1,0:T(8,128)(2,1)S(1)}, bf16[2,256,512]{2,1,0:T(8,128)(2,1)S(1)}, u32[]{:S(2)}, u32[]{:S(2)}) collective-permute-start(bf16[2,256,512]{2,1,0:T(8,128)(2,1)S(1)} %collective-permute-done.18.refs_4_), channel_id=1, source_target_pairs={{0,1},{1,0},{2,3},{3,2},{4,5},{5,4},{6,7},{7,6},{8,9},{9,8},{10,11... | collective-permute-start | bytes 1572872 | tf_op jit(solution)/shard_map/ppermute | solution.py:124
  125.6 3.6 collective-permute-start.40
  200.6 22.7 %collective-permute-start.43 = (bf16[2,2,256,512]{3,2,1,0:T(8,128)(2,1)}, bf16[2,2,256,512]{3,2,1,0:T(8,128)(2,1)}, u32[]{:S(2)}, u32[]{:S(2)}) collective-permute-start(bf16[2,2,256,512]{3,2,1,0:T(8,128)(2,1)} %get-tuple-element.75), channel_id=1, source_target_pairs={{0,1},{1,0},{2,3},{3,2},{4,5},{5,4},{6,7},{7,6},{8,9},{9,8},{10,11... | collective-permute-start | bytes 3145736 | tf_op jit(solution)/shard_map/ppermute | solution.py:124
  203.3 10.0 %collective-permute-start.45 = (bf16[2,2,256,512]{3,2,1,0:T(8,128)(2,1)}, bf16[2,2,256,512]{3,2,1,0:T(8,128)(2,1)}, u32[]{:S(2)}, u32[]{:S(2)}) collective-permute-start(bf16[2,2,256,512]{3,2,1,0:T(8,128)(2,1)} %get-tuple-element.78), channel_id=1, source_target_pairs={{0,1},{1,0},{2,3},{3,2},{4,5},{5,4},{6,7},{7,6},{8,9},{9,8},{10,11... | collective-permute-start | bytes 3145736 | tf_op jit(solution)/shard_map/ppermute | solution.py:124
  212.4 9.6 %collective-permute-start.49 = (bf16[8,40,1024]{2,1,0:T(8,128)(2,1)}, bf16[8,40,1024]{2,1,0:T(8,128)(2,1)}, u32[]{:S(2)}, u32[]{:S(2)}) collective-permute-start(bf16[8,40,1024]{2,1,0:T(8,128)(2,1)} %get-tuple-element.81), channel_id=1, source_target_pairs={{0,1},{1,0},{2,3},{3,2},{4,5},{5,4},{6,7},{7,6},{8,9},{9,8},{10,11... | collective-permute-start | bytes 1966088 | tf_op jit(solution)/shard_map/ppermute | solution.py:124
  212.8 69.8 %collective-permute-start.41 = (bf16[2,2,256,512]{3,2,1,0:T(8,128)(2,1)}, bf16[2,2,256,512]{3,2,1,0:T(8,128)(2,1)S(1)}, u32[]{:S(2)}, u32[]{:S(2)}) collective-permute-start(bf16[2,2,256,512]{3,2,1,0:T(8,128)(2,1)} %get-tuple-element.72), channel_id=1, source_target_pairs={{0,1},{1,0},{2,3},{3,2},{4,5},{5,4},{6,7},{7,6},{8,9},{9,8},{10,11... | collective-permute-start | bytes 3145736 | tf_op jit(solution)/shard_map/ppermute | solution.py:124
  212.9 33.3 %collective-permute-start.54 = (bf16[8,64,640]{2,1,0:T(8,128)(2,1)S(1)}, bf16[8,64,640]{2,1,0:T(8,128)(2,1)S(1)}, u32[]{:S(2)}, u32[]{:S(2)}) collective-permute-start(bf16[8,64,640]{2,1,0:T(8,128)(2,1)S(1)} %copy-done.29), channel_id=1, source_target_pairs={{0,1},{1,0},{2,3},{3,2},{4,5},{5,4},{6,7},{7,6},{8,9},{9,8},{10,11... | collective-permute-start | bytes 1966088 | tf_op jit(solution)/shard_map/ppermute | solution.py:124
  215.1 30.2 %collective-permute-start.46 = (bf16[2,256,512]{2,1,0:T(8,128)(2,1)S(1)}, bf16[2,256,512]{2,1,0:T(8,128)(2,1)S(1)}, u32[]{:S(2)}, u32[]{:S(2)}) collective-permute-start(bf16[2,256,512]{2,1,0:T(8,128)(2,1)S(1)} %fusion.24), channel_id=1, source_target_pairs={{0,2},{1,3},{2,0},{3,1},{4,6},{5,7},{6,4},{7,5},{8,10},{9,11},{10,... | collective-permute-start | bytes 1572872 | tf_op jit(solution)/shard_map/ppermute | solution.py:120
  223.2 29.8 %collective-permute-start.50 = (bf16[4,40,1024]{2,1,0:T(8,128)(2,1)S(1)}, bf16[4,40,1024]{2,1,0:T(8,128)(2,1)S(1)}, u32[]{:S(2)}, u32[]{:S(2)}) collective-permute-start(bf16[4,40,1024]{2,1,0:T(8,128)(2,1)S(1)} %add_convert_fusion.2), channel_id=1, source_target_pairs={{0,2},{1,3},{2,0},{3,1},{4,6},{5,7},{6,4},{7,5},{8,10},{9,11},{10,... | collective-permute-start | bytes 983048 | tf_op jit(solution)/shard_map/ppermute | solution.py:120
  225.1 58.9 %collective-permute-start.44 = (bf16[2,256,512]{2,1,0:T(8,128)(2,1)S(1)}, bf16[2,256,512]{2,1,0:T(8,128)(2,1)S(1)}, u32[]{:S(2)}, u32[]{:S(2)}) collective-permute-start(bf16[2,256,512]{2,1,0:T(8,128)(2,1)S(1)} %fusion.29), channel_id=1, source_target_pairs={{0,2},{1,3},{2,0},{3,1},{4,6},{5,7},{6,4},{7,5},{8,10},{9,11},{10,... | collective-permute-start | bytes 1572872 | tf_op jit(solution)/shard_map/ppermute | solution.py:120
  245.5 38.8 %collective-permute-start.47 = (bf16[2,256,512]{2,1,0:T(8,128)(2,1)S(1)}, bf16[2,256,512]{2,1,0:T(8,128)(2,1)S(1)}, u32[]{:S(2)}, u32[]{:S(2)}) collective-permute-start(bf16[2,256,512]{2,1,0:T(8,128)(2,1)S(1)} %fusion.27), channel_id=1, source_target_pairs={{8,4},{9,5},{10,6},{11,7},{12,8},{13,9},{14,10},{15,11},{24,20},{2... | collective-permute-start | bytes 1572872 | tf_op jit(solution)/shard_map/ppermute | solution.py:116
  246.3 40.4 %collective-permute-start.55 = (bf16[4,64,640]{2,1,0:T(8,128)(2,1)S(1)}, bf16[4,64,640]{2,1,0:T(8,128)(2,1)S(1)}, u32[]{:S(2)}, u32[]{:S(2)}) collective-permute-start(bf16[4,64,640]{2,1,0:T(8,128)(2,1)S(1)} %add_convert_fusion.1), channel_id=1, source_target_pairs={{0,2},{1,3},{2,0},{3,1},{4,6},{5,7},{6,4},{7,5},{8,10},{9,11},{10,... | collective-permute-start | bytes 983048 | tf_op jit(solution)/shard_map/ppermute | solution.py:120
  254.0 34.2 %collective-permute-start.53 = (bf16[40,1024]{1,0:T(8,128)(2,1)S(1)}, bf16[40,1024]{1,0:T(8,128)(2,1)S(1)}, u32[]{:S(2)}, u32[]{:S(2)}) collective-permute-start(bf16[40,1024]{1,0:T(8,128)(2,1)S(1)} %get-tuple-element.159), channel_id=1, source_target_pairs={{0,12},{1,13},{2,14},{3,15},{4,0},{5,1},{6,2},{7,3},{8,4},{9,5},{1... | collective-permute-start | bytes 245768 | tf_op jit(solution)/shard_map/ppermute | solution.py:108
  282.7 23.8 %collective-permute-start.52 = (bf16[40,1024]{1,0:T(8,128)(2,1)S(1)}, bf16[40,1024]{1,0:T(8,128)(2,1)S(1)}, u32[]{:S(2)}, u32[]{:S(2)}) collective-permute-start(bf16[40,1024]{1,0:T(8,128)(2,1)S(1)} %get-tuple-element.160), channel_id=1, source_target_pairs={{0,8},{1,9},{2,10},{3,11},{4,12},{5,13},{6,14},{7,15},{8,0},{9,1},... | collective-permute-start | bytes 245768 | tf_op jit(solution)/shard_map/ppermute | solution.py:108
  283.9 22.6 %collective-permute-start.51 = (bf16[40,1024]{1,0:T(8,128)(2,1)S(1)}, bf16[40,1024]{1,0:T(8,128)(2,1)S(1)}, u32[]{:S(2)}, u32[]{:S(2)}) collective-permute-start(bf16[40,1024]{1,0:T(8,128)(2,1)S(1)} %get-tuple-element.158), channel_id=1, source_target_pairs={{0,4},{1,5},{2,6},{3,7},{4,8},{5,9},{6,10},{7,11},{8,12},{9,13},{1... | collective-permute-start | bytes 245768 | tf_op jit(solution)/shard_map/ppermute | solution.py:108
  284.3 45.1 %collective-permute-start.42 = (bf16[2,256,512]{2,1,0:T(8,128)(2,1)S(1)}, bf16[2,256,512]{2,1,0:T(8,128)(2,1)S(1)}, u32[]{:S(2)}, u32[]{:S(2)}) collective-permute-start(bf16[2,256,512]{2,1,0:T(8,128)(2,1)S(1)} %fusion.35), channel_id=1, source_target_pairs={{0,2},{1,3},{2,0},{3,1},{4,6},{5,7},{6,4},{7,5},{8,10},{9,11},{10,... | collective-permute-start | bytes 1572872 | tf_op jit(solution)/shard_map/ppermute | solution.py:120
  286.7 42.6 %collective-permute-start.48 = (bf16[2,256,512]{2,1,0:T(8,128)(2,1)S(1)}, bf16[2,256,512]{2,1,0:T(8,128)(2,1)S(1)}, u32[]{:S(2)}, u32[]{:S(2)}) collective-permute-start(bf16[2,256,512]{2,1,0:T(8,128)(2,1)S(1)} %fusion.33), channel_id=1, source_target_pairs={{4,0},{5,1},{6,2},{7,3},{8,4},{9,5},{10,6},{11,7},{12,8},{13,9},{1... | collective-permute-start | bytes 1572872 | tf_op jit(solution)/shard_map/ppermute | solution.py:116
  288.2 33.0 %collective-permute-start.58 = (bf16[64,640]{1,0:T(8,128)(2,1)S(1)}, bf16[64,640]{1,0:T(8,128)(2,1)S(1)}, u32[]{:S(2)}, u32[]{:S(2)}) collective-permute-start(bf16[64,640]{1,0:T(8,128)(2,1)S(1)} %get-tuple-element.156), channel_id=1, source_target_pairs={{0,12},{1,13},{2,14},{3,15},{4,0},{5,1},{6,2},{7,3},{8,4},{9,5},{1... | collective-permute-start | bytes 245768 | tf_op jit(solution)/shard_map/ppermute | solution.py:108
  306.5 20.3 %collective-permute-start.57 = (bf16[64,640]{1,0:T(8,128)(2,1)S(1)}, bf16[64,640]{1,0:T(8,128)(2,1)S(1)}, u32[]{:S(2)}, u32[]{:S(2)}) collective-permute-start(bf16[64,640]{1,0:T(8,128)(2,1)S(1)} %get-tuple-element.157), channel_id=1, source_target_pairs={{0,8},{1,9},{2,10},{3,11},{4,12},{5,13},{6,14},{7,15},{8,0},{9,1},... | collective-permute-start | bytes 245768 | tf_op jit(solution)/shard_map/ppermute | solution.py:108
  306.5 22.7 %collective-permute-start.56 = (bf16[64,640]{1,0:T(8,128)(2,1)S(1)}, bf16[64,640]{1,0:T(8,128)(2,1)S(1)}, u32[]{:S(2)}, u32[]{:S(2)}) collective-permute-start(bf16[64,640]{1,0:T(8,128)(2,1)S(1)} %get-tuple-element.155), channel_id=1, source_target_pairs={{0,4},{1,5},{2,6},{3,7},{4,8},{5,9},{6,10},{7,11},{8,12},{9,13},{1... | collective-permute-start | bytes 245768 | tf_op jit(solution)/shard_map/ppermute | solution.py:108
  338.8 7.2 %collective-permute-start.60 = (bf16[4,48,512]{2,1,0:T(8,128)(2,1)S(1)}, bf16[4,48,512]{2,1,0:T(8,128)(2,1)S(1)}, u32[]{:S(2)}, u32[]{:S(2)}) collective-permute-start(bf16[4,48,512]{2,1,0:T(8,128)(2,1)S(1)} %add_convert_fusion.3), channel_id=1, source_target_pairs={{0,2},{1,3},{2,0},{3,1},{4,6},{5,7},{6,4},{7,5},{8,10},{9,11},{10,... | collective-permute-start | bytes 589832 | tf_op jit(solution)/shard_map/ppermute | solution.py:120
  346.1 8.7 %collective-permute-start.64 = (bf16[48,512]{1,0:T(8,128)(2,1)S(1)}, bf16[48,512]{1,0:T(8,128)(2,1)S(1)}, u32[]{:S(2)}, u32[]{:S(2)}) collective-permute-start(bf16[48,512]{1,0:T(8,128)(2,1)S(1)} %get-tuple-element.166), channel_id=1, source_target_pairs={{0,12},{1,13},{2,14},{3,15},{4,0},{5,1},{6,2},{7,3},{8,4},{9,5},{1... | collective-permute-start | bytes 147464 | tf_op jit(solution)/shard_map/ppermute | solution.py:108
  346.2 10.6 %collective-permute-start.63 = (bf16[48,512]{1,0:T(8,128)(2,1)S(1)}, bf16[48,512]{1,0:T(8,128)(2,1)S(1)}, u32[]{:S(2)}, u32[]{:S(2)}) collective-permute-start(bf16[48,512]{1,0:T(8,128)(2,1)S(1)} %get-tuple-element.167), channel_id=1, source_target_pairs={{0,8},{1,9},{2,10},{3,11},{4,12},{5,13},{6,14},{7,15},{8,0},{9,1},... | collective-permute-start | bytes 147464 | tf_op jit(solution)/shard_map/ppermute | solution.py:108
  347.3 9.5 %collective-permute-start.62 = (bf16[48,512]{1,0:T(8,128)(2,1)S(1)}, bf16[48,512]{1,0:T(8,128)(2,1)S(1)}, u32[]{:S(2)}, u32[]{:S(2)}) collective-permute-start(bf16[48,512]{1,0:T(8,128)(2,1)S(1)} %get-tuple-element.165), channel_id=1, source_target_pairs={{0,4},{1,5},{2,6},{3,7},{4,8},{5,9},{6,10},{7,11},{8,12},{9,13},{1... | collective-permute-start | bytes 147464 | tf_op jit(solution)/shard_map/ppermute | solution.py:108
  351.3 9.7 %collective-permute-start.61 = (bf16[40,1024]{1,0:T(8,128)(2,1)S(1)}, bf16[40,1024]{1,0:T(8,128)(2,1)S(1)}, u32[]{:S(2)}, u32[]{:S(2)}) collective-permute-start(bf16[40,1024]{1,0:T(8,128)(2,1)S(1)} %copy-done.67), channel_id=1, source_target_pairs={{0,16},{16,0},{1,17},{17,1},{2,18},{18,2},{3,19},{19,3},{4,20},{20... | collective-permute-start | bytes 245768 | tf_op jit(solution)/shard_map/ppermute | solution.py:171
  354.8 5.4 %collective-permute-start.66 = (bf16[64,640]{1,0:T(8,128)(2,1)S(1)}, bf16[64,640]{1,0:T(8,128)(2,1)S(1)}, u32[]{:S(2)}, u32[]{:S(2)}) collective-permute-start(bf16[64,640]{1,0:T(8,128)(2,1)S(1)} %fusion.121), channel_id=1, source_target_pairs={{0,16},{16,0},{1,17},{17,1},{2,18},{18,2},{3,19},{19,3},{4,20},{20... | collective-permute-start | bytes 245768 | tf_op jit(solution)/shard_map/ppermute | solution.py:171
  354.8 17.5 %collective-permute-start.67 = (bf16[64,4096]{1,0:T(8,128)(2,1)S(1)}, bf16[64,4096]{1,0:T(8,128)(2,1)S(1)}, u32[]{:S(2)}, u32[]{:S(2)}) collective-permute-start(bf16[64,4096]{1,0:T(8,128)(2,1)S(1)} %bitcast.169), channel_id=1, source_target_pairs={{0,16},{16,0},{1,17},{17,1},{2,18},{18,2},{3,19},{19,3},{4,20},{20... | collective-permute-start | bytes 1572872 | tf_op jit(solution)/shard_map/ppermute | solution.py:171
  356.8 13.9 %collective-permute-start.65 = (bf16[48,512]{1,0:T(8,128)(2,1)S(1)}, bf16[48,512]{1,0:T(8,128)(2,1)S(1)}, u32[]{:S(2)}, u32[]{:S(2)}) collective-permute-start(bf16[48,512]{1,0:T(8,128)(2,1)S(1)} %fusion.135), channel_id=1, source_target_pairs={{0,16},{16,0},{1,17},{17,1},{2,18},{18,2},{3,19},{19,3},{4,20},{20... | collective-permute-start | bytes 147464 | tf_op jit(solution)/shard_map/ppermute | solution.py:171
  (101 other events, 809.5 us)
Sparse Core Ops, SparseCore 0:
  11.3 103.8 all-gather.2
  177.7 141.2 reduce-scatter.1
